TPU v7x, 256 devices: a whole 4x4x8 slice. The times are simulated.
256 devices in a mesh: tower: 2 (over x_lo), blk: 128 (over y, x_hi, z, core).
Axes of the slice: x: 4 (x_hi: 2, x_lo: 2; x = x_hi * 2 + x_lo), y: 4, z: 8, core: 2. Of those that a mesh axis runs over, the one named last changes fastest.
Arguments:
- embeddings: bfloat16 [2, 16384, 896], P('tower', 'blk'), may hold values from -0.25 to 0.25
- pair: int32 [16384], P('blk'), may hold values from 0 to 16383, as said below
- logit_scale: float32 [], replicated, may hold values from 16 to 32
Outputs:
- emb_grad: bfloat16 [2, 16384, 896], P('tower', 'blk')
- loss: float32 [2], P('tower')
- scale_grad: float32 [2], P('tower')
Inputs may be any that keep to these rules, and one draw needn't show every extreme that they name: pair is a permutation: every text index appears once.
All inputs are finite; a program needn't handle non-finite values.
Results may differ from a plain program's by a relative error of at most 0.0054.
Values may be sent and summed in bfloat16 or wider, within the bound.
A program may use at most 128 MiB of HBM per device.

v0:
```python
import math

import jax
import jax.numpy as jnp
from jax import lax
from jax.sharding import PartitionSpec as P

eps = 1e-06


def partner_2(x, axis, distance):
    return lax.ppermute(x, axis, [(i, i ^ 1 << distance) for i in range(lax.axis_size(axis))])


def tile_terms(unit_rows, columns, first_row, scale_value, targets):
    scores = scale_value * lax.dot_general(
        unit_rows, columns, (((1,), (1,)), ((), ())), preferred_element_type=jnp.float32
    )
    exponent = jnp.exp(scores - scale_value)
    column_ids = first_row + jnp.arange(columns.shape[0], dtype=jnp.int32)
    positive = column_ids[None, :] == targets[:, None]
    return (scores, exponent, positive)


def fold_stats(unit_rows, received, first_row, scale_value, targets, wanted):
    count = received.shape[0]
    block_len = math.gcd(count, wanted)
    block_total = count // block_len

    def per_block(running, block_index):
        columns = lax.dynamic_slice_in_dim(received, block_index * block_len, block_len, 0)
        scores, exponent, positive = tile_terms(
            unit_rows, columns, first_row + block_index * block_len, scale_value, targets
        )
        return (
            (
                running[0] + jnp.sum(exponent, axis=1),
                running[1] + jnp.sum(exponent * scores, axis=1),
                running[2] + jnp.sum(jnp.where(positive, scores, 0.0), axis=1),
            ),
            None,
        )

    zeros_vec = jnp.zeros((unit_rows.shape[0],), jnp.float32)
    result, _ = lax.scan(
        per_block, (zeros_vec, zeros_vec, zeros_vec), jnp.arange(block_total, dtype=jnp.int32)
    )
    return result


def body(embeddings, pair, logit_scale):
    widened = embeddings[0].astype(jnp.float32)
    lengths = jnp.sqrt(jnp.sum(widened * widened, axis=1) + eps)
    unit32 = widened / lengths[:, None]
    unit_rows = unit32.astype(jnp.bfloat16)
    row_count = unit_rows.shape[0]
    width = unit_rows.shape[1]
    blk_count = lax.axis_size("blk")
    total_rows = row_count * blk_count
    my_index = lax.axis_index("blk")
    section = lax.axis_index("tower")
    partner = partner_2(unit_rows, "tower", 0)
    pair_all = lax.all_gather(pair, "blk", axis=0, tiled=True)
    inverse = (
        jnp.zeros((total_rows,), jnp.int32)
        .at[pair_all]
        .set(jnp.arange(total_rows, dtype=jnp.int32))
    )
    inverse_local = lax.dynamic_slice_in_dim(inverse, my_index * row_count, row_count, 0)
    targets = jnp.where(section == 0, pair, inverse_local)
    group_size = 1
    for option in range(1, max(1, 1024 // row_count) + 1):
        if blk_count % option == 0:
            group_size = option
    wanted = row_count * group_size
    gathered = lax.all_gather(partner, "blk", axis=0, tiled=True)
    own_denom, own_expected, own_matched = fold_stats(
        unit_rows, gathered, 0, logit_scale, targets, wanted
    )
    loss_part = jnp.sum(logit_scale + jnp.log(own_denom) - own_matched)
    temper_part = jnp.sum(own_expected / own_denom - own_matched)
    denom_all = lax.all_gather(own_denom, ("tower", "blk"), axis=0, tiled=True)
    loss_total, temper_total = lax.psum((loss_part, temper_part), "blk")
    denom_pair = denom_all.reshape(2, total_rows)
    other_denom = jnp.where(section == 0, denom_pair[1], denom_pair[0])
    block_len = math.gcd(total_rows, wanted)
    block_total = total_rows // block_len

    def grad_block(accumulated, block_index):
        columns = lax.dynamic_slice_in_dim(gathered, block_index * block_len, block_len, 0)
        column_denom = lax.dynamic_slice_in_dim(other_denom, block_index * block_len, block_len, 0)
        scores, exponent, positive = tile_terms(
            unit_rows, columns, block_index * block_len, logit_scale, targets
        )
        weights = 0.5 * (
            exponent / own_denom[:, None] + exponent / column_denom[None, :]
        ) - jnp.where(positive, 1.0, 0.0)
        return (
            accumulated
            + jnp.dot(weights.astype(jnp.bfloat16), columns, preferred_element_type=jnp.float32),
            None,
        )

    accumulated, _ = lax.scan(
        grad_block,
        jnp.zeros((row_count, width), jnp.float32),
        jnp.arange(block_total, dtype=jnp.int32),
    )
    grads = accumulated * logit_scale
    inner = jnp.sum(unit32 * grads, axis=1)
    emb_grad = ((grads - unit32 * inner[:, None]) / lengths[:, None]).astype(jnp.bfloat16)
    loss = loss_total / (2 * total_rows)
    scale_grad = temper_total / logit_scale / (2 * total_rows)
    return (emb_grad[None], loss[None], scale_grad[None])


def solution(mesh):
    placed = (P("tower", "blk", None), P("blk"), P())
    return jax.shard_map(
        body,
        mesh=mesh,
        in_specs=placed,
        out_specs=(P("tower", "blk", None), P("tower"), P("tower")),
        check_vma=False,
    )
```

profile of v0, /device:TPU:2, one launch (start us, length us, event | category | flops | bytes accessed | tf_op | source)
XLA Modules:
  0.0 1094.2 jit_solution(16977791897774775483)
XLA Ops:
  11.7 5.1 collective-permute-done
  18.2 184.2 %all-gather = s32[128,1,128]{2,1,0:T(1,128)S(1)} all-gather(s32[1,1,128]{2,1,0:T(1,128)} %bitcast.43), channel_id=1, replica_groups=mesh['tower'=2,'blk'=128] {'blk'}, dimensions={0}, use_global_device_ids=true | all-gather | bytes 66048 | tf_op jit(solution)/shard_map/all_gather | solution.py:63
  202.4 60.3 %scatter_custom_fusion = s32[16384]{0:T(1024)S(1)} fusion(s32[16384]{0:T(1024)S(1)} %compare_select_fusion, s32[16384]{0:T(1024)S(1)} %iota.21, s32[]{:T(128)} %constant.11.clone.1), kind=kCustom, calls=%fused_computation.49 | custom fusion | bytes 65540 | tf_op jit(solution)/shard_map/scatter | solution.py:67
  262.9 66.8 %while.26 = (s32[]{:T(128)}, f32[128]{0:T(128)S(1)}, f32[128]{0:T(128)S(1)}, f32[128]{0:T(128)S(1)}, f32[]{:T(128)}, /*index=5*/s32[16]{0:T(128)S(1)}, bf16[1638...) while((s32[]{:T(128)}, f32[128]{0:T(128)S(1)}, ...), condition=%wide.region_6.7_spmd.clone, body=%wide.region_2.6_spmd.clone.sunk | while | flops 235931008 | bytes 2080466 | solution.py:45
  264.1 2.9 select_reduce_fusion.2
  268.3 2.9 select_reduce_fusion.2
  276.7 2.9 select_reduce_fusion.2
  285.0 2.9 select_reduce_fusion.2
  293.4 2.9 select_reduce_fusion.2
  301.7 2.9 select_reduce_fusion.2
  310.1 2.9 select_reduce_fusion.2
  318.4 2.9 select_reduce_fusion.2
  326.8 2.9 select_reduce_fusion.2
  329.7 298.9 %all-gather.1 = f32[256,1,128]{2,1,0:T(1,128)S(1)} all-gather(f32[1,1,128]{2,1,0:T(1,128)S(1)} %bitcast.42), channel_id=1, replica_groups=mesh['tower'=2,'blk'=128] {'tower','blk'}, dimensions={0}, use_global_device_ids=true | all-gather | bytes 131584 | tf_op jit(solution)/shard_map/all_gather | solution.py:82
  628.7 87.8 %while.27 = (s32[]{:T(128)}, f32[128,896]{1,0:T(8,128)S(1)}, f32[]{:T(128)}, s32[16]{0:T(128)S(1)}, bf16[16384,896]{1,0:T(8,128)(2,1)}, /*index=5*/bf16[128,896]...) while((s32[]{:T(128)}, f32[128,896]{1,0:T(8,128)S(1)}, ...), condition=%wide.region_8.9_spmd.clone, body=%wide.region_7.8_spmd.clone.sunk | while | flops 471303168 | bytes 4840656 | solution.py:104
  629.9 4.2 fusion.68
  635.4 4.2 fusion.68
  640.9 4.2 fusion.68
  646.4 4.2 fusion.68
  651.9 4.3 fusion.68
  657.4 4.2 fusion.68
  662.9 4.2 fusion.68
  668.4 4.2 fusion.68
  673.9 4.2 fusion.68
  679.4 4.2 fusion.68
  684.9 4.2 fusion.68
  690.4 4.2 fusion.68
  695.8 4.2 fusion.68
  701.3 4.2 fusion.68
  706.8 4.2 fusion.68
  712.3 4.2 fusion.68
  718.2 365.6 %all-reduce = (f32[]{:T(128)}, f32[]{:T(128)}) all-reduce(f32[]{:T(128)} %get-tuple-element.167, f32[]{:T(128)} %get-tuple-element.166), channel_id=1, replica_groups=mesh['tower'=2,'blk'=128] {'blk'}, use_global_device_ids=true, to_apply=%region_11.12 | all-reduce | flops 2 | bytes 16 | tf_op jit(solution)/shard_map/psum | solution.py:83
  (143 shorter events, 46.6 us)
Async XLA Ops:
  7.2 255.7 %all-gather.4.cloned.1.call-start = ((), (), s32[]{:S(2)}) async-start(), calls=%async_computation | async-start | bytes 29589504 | tf_op jit(solution)/shard_map/all_gather | solution.py:76
  9.3 7.4 collective-permute-start
  16.8 0.7 copy-start.1
  262.9 453.6 %copy-start = (bf16[1,128,896]{2,1,0:T(8,128)(2,1)S(1)}, bf16[1,128,896]{2,1,0:T(8,128)(2,1)}, u32[]{:S(2)}) copy-start(bf16[1,128,896]{2,1,0:T(8,128)(2,1)} %param.7) | copy-start | bytes 688132
Sparse Core Ops, SparseCore 0:
  17.6 199.2 all-gather.3
where the time goes:
time: 1100 us; the launch traced here: 1090 us
  blocking collectives  849 us (77%)
  matrix products  113 us (10%)
  local copies, waits for them, and re-layouts  79.9 us (7%)
  loops' own time  22.3 us (2%)
  between operations  18.3 us (2%)
    psum x1, blocking collectives, body(): loss_total, temper_total = lax.psum((loss_part, temper_part), 'blk')  366 us
    all_gather x1, blocking collectives, body(): denom_all = lax.all_gather(own_denom, ('tower', 'blk'), axis=0, tiled=True)  299 us
    all_gather x1, blocking collectives, body(): pair_all = lax.all_gather(pair, 'blk', axis=0, tiled=True)  184 us
    dot_general x16, matrix products, grad_block(): jnp.dot(weights.astype(jnp.bfloat16), columns, preferred_element_type=jnp...  67.1 us
    scatter x1, local copies, waits for them, and re-layouts, body(): inverse = jnp.zeros((total_rows,), jnp.int32).at[pair_all].set(jnp.arange...  60.3 us
    dot_general x16, matrix products, tile_terms(): lax.dot_general(unit_rows, columns, (((1,), (1,)), ((), ())), preferred_e...  45.9 us
  transfers between devices with their start and end apart: 2, of which 1 were waited for; matrix products, arithmetic and copies ran while one was open for 6% of the time, Pallas kernels for 0%

commit v1 on v0

v1 whole, which is shorter than its diff:
```python
import jax
import jax.numpy as jnp
from jax import lax
from jax.experimental import pallas as pl
from jax.experimental.pallas import tpu as pltpu
from jax.sharding import PartitionSpec as P

eps = 1e-06
TOK = 128
D = 896
TOKENS = 16384
NY, NXH, NZ, NC = 4, 2, 8, 2
f32 = jnp.float32
bf16 = jnp.bfloat16
MESH = pl.DeviceIdType.MESH


def device(t, y, xh, z, c):
    return (t, ((y * NXH + xh) * NZ + z) * NC + c)


def kernel(
    scale_ref, emb_ref, pair_ref,
    out_ref, loss_ref, sgrad_ref,
    own, images, texts, texts_t, pairs, exps, weights,
    text_part, text_send, text_recv, image_part, image_send, image_sib, image_recv,
    stat_send, z_img_all, z_txt_all, e_img, scal_send, scal_z, scal_p, fin_send, fin_recv,
    s_txt, r_txt, s_img, r_img, s_sib, r_sib, s_pair, r_pair, s_x, r_x,
    s_zi, r_zi, s_zt, r_zt, s_sz, r_sz, s_sp, r_sp,
    s_rt, r_rt, s_ri, r_ri, s_rs, r_rs, s_fin, r_fin,
):
    t = lax.axis_index("tower")
    b = lax.axis_index("blk")
    c = b % 2
    z = (b // 2) % 8
    xh = (b // 16) % 2
    y = b // 32
    is_text = t == 1
    is_root = c == t
    line_rank = z * 2 + c
    plane_rank = (t * 4 + y) * 2 + xh
    text_index = y * 2 + xh
    scale = scale_ref[0]

    line_peers = [
        device(t, y, xh, (z + dz) % 8, (c + dc) % 2)
        for dz in (4, 3, 5, 2, 6, 1, 7, 0) for dc in (0, 1) if dz or dc
    ]
    plane_peers = [
        device((t + dt) % 2, (y + dy) % 4, (xh + dx) % 2, z, c)
        for dy in (2, 1, 3, 0) for dx in (1, 0) for dt in (0, 1) if dy or dx or dt
    ]
    sibling = device(t, y, xh, z, 1 - c)
    ring_peers = [device(t, y, xh, (z + dz) % 8, c) for dz in (4, 3, 5, 2, 6, 1, 7)]

    def send(src, dst, ssem, rsem, target):
        pltpu.make_async_remote_copy(
            src_ref=src, dst_ref=dst, send_sem=ssem, recv_sem=rsem,
            device_id=target, device_id_type=MESH,
        ).start()

    def landed(dst, rsem):
        pltpu.make_async_copy(dst, dst, rsem).wait()

    barrier = pltpu.get_barrier_semaphore()
    for peer in line_peers + plane_peers:
        pl.semaphore_signal(barrier, inc=1, device_id=peer, device_id_type=MESH)

    wide = emb_ref[0].astype(f32)
    lengths = jnp.sqrt(jnp.sum(wide * wide, axis=1, keepdims=True) + eps)
    unit = (wide / lengths).astype(bf16)
    own[...] = unit

    @pl.when(is_text)
    def _():
        texts[text_index] = unit

    @pl.when(jnp.logical_and(t == 0, c == 0))
    def _():
        images[z] = unit

    @pl.when(is_root)
    def _():
        pairs[z] = pair_ref[...]

    pl.semaphore_wait(barrier, 30)

    @pl.when(jnp.logical_and(t == 0, c == 1))
    def _():
        send(own, images.at[z], s_x.at[0], r_x.at[0], device(1, y, xh, z, c))

    @pl.when(is_root)
    def _():
        for k, peer in enumerate(line_peers):
            send(pair_ref, pairs.at[z], s_pair.at[k], r_pair.at[z], peer)

    @pl.when(is_text)
    def _():
        for k, peer in enumerate(plane_peers):
            send(own, texts.at[text_index], s_txt.at[k], r_txt.at[text_index], peer)

    @pl.when(jnp.logical_and(t == 1, c == 1))
    def _():
        landed(images.at[z], r_x.at[0])

    @pl.when(is_root)
    def _():
        for k, peer in enumerate(ring_peers):
            send(images.at[z], images.at[z], s_img.at[k], r_img.at[z], peer)
        send(images.at[z], images.at[z], s_sib.at[0], r_sib.at[z], sibling)
        for k, dz in enumerate((1, 7, 2, 6, 3, 5, 4)):
            other = (z + dz) % 8
            landed(images.at[other], r_img.at[other])
            send(images.at[other], images.at[other], s_sib.at[1 + k], r_sib.at[other], sibling)
            landed(pairs.at[other], r_pair.at[other])

    @pl.when(jnp.logical_not(is_root))
    def _():
        for dz in (0, 1, 7, 2, 6, 3, 5, 4):
            other = (z + dz) % 8
            landed(images.at[other], r_sib.at[other])
            landed(pairs.at[other], r_pair.at[other])

    def text_landed(dy, dx):
        other = ((y + dy) % 4) * 2 + (xh + dx) % 2
        landed(texts.at[other], r_txt.at[other])

    for dy in range(4):
        for dx in range(2):
            if dy == 0 and dx == 0:
                @pl.when(jnp.logical_not(is_text))
                def _():
                    text_landed(0, 0)
            else:
                text_landed(dy, dx)

    pair_row = jnp.concatenate([pairs[k][0:1] for k in range(8)], axis=1)
    sub_ids = lax.broadcasted_iota(jnp.int32, (TOK, 1), 0)

    def first_id(block):
        return ((block * 8 + z) * 2 + c) * TOK

    all_images = images[...].reshape(8 * TOK, D)

    def stats(block, carry):
        zi, ei, pi = carry
        rows = texts[block]
        dots = lax.dot_general(rows, all_images, (((1,), (1,)), ((), ())), preferred_element_type=f32)
        scores = scale * dots
        ex = jnp.exp(scores - scale)
        exps[block] = ex
        es = ex * scores
        match = pair_row == first_id(block) + sub_ids
        zi = zi + jnp.sum(ex, axis=0, keepdims=True)
        ei = ei + jnp.sum(es, axis=0, keepdims=True)
        pi = pi + jnp.sum(jnp.where(match, scores, 0.0), axis=0, keepdims=True)
        zr = ex[:, 0:TOK]
        er = es[:, 0:TOK]
        for k in range(1, 8):
            zr = zr + ex[:, k * TOK:(k + 1) * TOK]
            er = er + es[:, k * TOK:(k + 1) * TOK]
        stat_send[1, pl.ds(block, 1), :] = jnp.sum(zr.T, axis=0, keepdims=True)
        e_img[1, pl.ds(block, 1), :] = jnp.sum(er.T, axis=0, keepdims=True)
        texts_t[block] = rows.astype(f32).T.astype(bf16)
        return zi, ei, pi

    zero = jnp.zeros((1, 8 * TOK), f32)
    zi, ei, pi = lax.fori_loop(0, 8, stats, (zero, zero, zero))
    for k in range(8):
        stat_send[0, k:k + 1, :] = zi[:, k * TOK:(k + 1) * TOK]
        e_img[0, k:k + 1, :] = ei[:, k * TOK:(k + 1) * TOK]

    for k, peer in enumerate(line_peers):
        send(stat_send.at[0], z_img_all.at[line_rank], s_zi.at[k], r_zi.at[line_rank], peer)
    for k, peer in enumerate(plane_peers):
        send(stat_send.at[1], z_txt_all.at[plane_rank], s_zt.at[k], r_zt.at[plane_rank], peer)
    z_img_all[line_rank] = stat_send[0]
    z_txt_all[plane_rank] = stat_send[1]

    def line_others():
        return [((z + dz) % 8) * 2 + (c + dc) % 2 for dz in range(8) for dc in range(2) if dz or dc]

    def plane_others():
        return [
            (((t + dt) % 2) * 4 + (y + dy) % 4) * 2 + (xh + dx) % 2
            for dy in range(4) for dx in range(2) for dt in range(2) if dy or dx or dt
        ]

    for other in line_others():
        landed(z_img_all.at[other], r_zi.at[other])
    for other in plane_others():
        landed(z_txt_all.at[other], r_zt.at[other])
    z_img = jnp.sum(z_img_all[...], axis=0)
    z_txt = jnp.sum(z_txt_all[...], axis=0)

    half_img = 0.5 / z_img
    half_txt = 0.5 / z_txt
    stat_send[2] = half_txt
    img_row = jnp.concatenate([half_img[k:k + 1] for k in range(8)], axis=1)

    def weigh(block, _):
        column = jnp.broadcast_to(stat_send[2, pl.ds(block, 1), :], (TOK, TOK)).T
        ids = first_id(block) + sub_ids
        for k in range(8):
            lanes = slice(k * TOK, (k + 1) * TOK)
            match = pair_row[:, lanes] == ids
            value = exps[block, :, lanes] * (img_row[:, lanes] + column)
            weights[block, :, lanes] = (value - jnp.where(match, 1.0, 0.0)).astype(bf16)
        return 0

    lax.fori_loop(0, 8, weigh, 0)

    lane = lax.broadcasted_iota(jnp.int32, (8, TOK), 1)

    def total(x):
        return jnp.sum(jnp.sum(x, axis=0, keepdims=True), axis=1, keepdims=True)

    log_img = total(jnp.log(z_img))
    log_txt = total(jnp.log(z_txt))
    t_img = total(e_img[0] / z_img)
    t_txt = total(e_img[1] / z_txt)
    matched = jnp.sum(pi, axis=1, keepdims=True)
    scal_send[0] = jnp.where(
        lane == 0, log_txt,
        jnp.where(lane == 1, t_img, jnp.where(lane == 2, t_txt, jnp.where(lane == 3, matched, 0.0))),
    )
    for k, peer in enumerate(line_peers):
        send(scal_send.at[0], scal_z.at[line_rank], s_sz.at[k], r_sz.at[line_rank], peer)
    scal_z[line_rank] = scal_send[0]

    def text_block(step, _):
        block = (text_index + 4 + step) % 8
        part = jnp.dot(weights[block], all_images, preferred_element_type=f32)
        text_part[block] = part
        text_send[block] = part.astype(bf16)

        @pl.when(jnp.logical_or(block != text_index, t == 0))
        def _():
            send(
                text_send.at[block], text_recv.at[plane_rank], s_rt.at[block], r_rt.at[plane_rank],
                device(1, block // 2, block % 2, z, c),
            )
        return 0

    lax.fori_loop(0, 8, text_block, 0)

    def image_pair(p, _):
        acc = jnp.zeros((D, 2 * TOK), f32)
        lanes = pl.ds(pl.multiple_of(p * 2 * TOK, 2 * TOK), 2 * TOK)
        for k in range(8):
            acc = acc + jnp.dot(texts_t[k], weights[k, :, lanes], preferred_element_type=f32)
        for h in range(2):
            image_part[2 * p + h] = acc[:, h * TOK:(h + 1) * TOK]

        @pl.when(jnp.logical_not(is_root))
        def _():
            for h in range(2):
                image_send[2 * p + h] = acc[:, h * TOK:(h + 1) * TOK].astype(bf16)
                send(
                    image_send.at[2 * p + h], image_sib.at[2 * p + h], s_rs.at[2 * p + h], r_rs.at[2 * p + h],
                    sibling,
                )
        return 0

    lax.fori_loop(0, 4, image_pair, 0)

    @pl.when(is_root)
    def _():
        def forward(step, _):
            block = (z + 4 + step) % 8
            landed(image_sib.at[block], r_rs.at[block])
            both = image_part[block] + image_sib[block].astype(f32)
            image_part[block] = both
            image_send[block] = both.astype(bf16)

            @pl.when(block != z)
            def _():
                send(
                    image_send.at[block], image_recv.at[z], s_ri.at[block], r_ri.at[z],
                    device(t, y, xh, block, c),
                )
            return 0
        lax.fori_loop(0, 8, forward, 0)

    for other in line_others():
        landed(scal_z.at[other], r_sz.at[other])
    line_sum = jnp.sum(scal_z[...], axis=0)
    scal_send[1] = jnp.where(lane == 4, log_img, line_sum)
    for k, peer in enumerate(plane_peers):
        send(scal_send.at[1], scal_p.at[plane_rank], s_sp.at[k], r_sp.at[plane_rank], peer)
    scal_p[plane_rank] = scal_send[1]

    def finish(grads):
        unit32 = wide / lengths
        grads = scale * grads
        inner = jnp.sum(unit32 * grads, axis=1, keepdims=True)
        out_ref[0] = ((grads - unit32 * inner) / lengths).astype(bf16)

    @pl.when(is_text)
    def _():
        acc = text_part[text_index]
        for other in plane_others():
            landed(text_recv.at[other], r_rt.at[other])
            acc = acc + text_recv[other].astype(f32)
        finish(acc)

    @pl.when(is_root)
    def _():
        acc = image_part[z]
        for dz in range(1, 8):
            other = (z + dz) % 8
            landed(image_recv.at[other], r_ri.at[other])
            acc = acc + image_recv[other].astype(f32)

        @pl.when(is_text)
        def _():
            fin_send[...] = acc.astype(bf16)
            send(fin_send, fin_recv, s_fin.at[0], r_fin.at[0], device(0, y, xh, z, c))

        @pl.when(jnp.logical_not(is_text))
        def _():
            finish(acc.T)

    @pl.when(jnp.logical_and(t == 0, c == 1))
    def _():
        landed(fin_recv, r_fin.at[0])
        finish(fin_recv[...].astype(f32).T)

    for other in plane_others():
        landed(scal_p.at[other], r_sp.at[other])
    all_sum = jnp.sum(scal_p[...], axis=0)

    def pick(k):
        return jnp.sum(jnp.where(lane[0:1] == k, all_sum[0:1], 0.0))

    log_txt_all = jnp.sum(jnp.where(lane[0:1] == 0, line_sum[0:1], 0.0))
    log_all = jnp.where(is_text, log_txt_all, pick(4))
    t_all = jnp.where(is_text, pick(2), pick(1))
    p_all = pick(3)
    loss_ref[0] = (scale * TOKENS + log_all - p_all) * (1.0 / (2 * TOKENS))
    sgrad_ref[0] = (t_all - p_all) / scale * (1.0 / (2 * TOKENS))

    def left(src, sem):
        pltpu.make_async_copy(src, src, sem).wait()

    for k in range(15):
        left(stat_send.at[0], s_zi.at[k])
        left(stat_send.at[1], s_zt.at[k])
        left(scal_send.at[0], s_sz.at[k])
        left(scal_send.at[1], s_sp.at[k])

    @pl.when(is_text)
    def _():
        for k in range(15):
            left(own, s_txt.at[k])

    @pl.when(jnp.logical_and(t == 0, c == 1))
    def _():
        left(own, s_x.at[0])

    @pl.when(jnp.logical_and(t == 1, c == 1))
    def _():
        left(fin_send, s_fin.at[0])

    @pl.when(is_root)
    def _():
        for k in range(15):
            left(pair_ref, s_pair.at[k])
        for k in range(7):
            left(own, s_img.at[k])
        for k in range(8):
            left(own, s_sib.at[k])
        for dz in range(1, 8):
            block = (z + dz) % 8
            left(image_send.at[block], s_ri.at[block])

    @pl.when(jnp.logical_not(is_root))
    def _():
        for k in range(8):
            left(image_send.at[k], s_rs.at[k])

    for k in range(8):
        @pl.when(jnp.logical_or(k != text_index, t == 0))
        def _():
            left(text_send.at[k], s_rt.at[k])


def body(embeddings, pair, logit_scale):
    vmem = pl.BlockSpec(memory_space=pltpu.VMEM)
    smem = pl.BlockSpec(memory_space=pltpu.SMEM)
    dma = pltpu.SemaphoreType.DMA
    sems = [15, 8, 7, 8, 8, 8, 15, 8, 1, 1, 15, 16, 15, 16, 15, 16, 15, 16, 8, 16, 8, 8, 8, 8, 1, 1]
    emb_grad, loss, scale_grad = pl.pallas_call(
        kernel,
        out_shape=(
            jax.ShapeDtypeStruct((1, TOK, D), bf16),
            jax.ShapeDtypeStruct((1,), f32),
            jax.ShapeDtypeStruct((1,), f32),
        ),
        in_specs=[smem, vmem, vmem],
        out_specs=(vmem, smem, smem),
        scratch_shapes=[
            pltpu.VMEM((TOK, D), bf16),
            pltpu.VMEM((8, TOK, D), bf16),
            pltpu.VMEM((8, TOK, D), bf16),
            pltpu.VMEM((8, D, TOK), bf16),
            pltpu.VMEM((8, 8, TOK), jnp.int32),
            pltpu.VMEM((8, TOK, 8 * TOK), f32),
            pltpu.VMEM((8, TOK, 8 * TOK), bf16),
            pltpu.VMEM((8, TOK, D), f32),
            pltpu.VMEM((8, TOK, D), bf16),
            pltpu.VMEM((16, TOK, D), bf16),
            pltpu.VMEM((8, D, TOK), f32),
            pltpu.VMEM((8, D, TOK), bf16),
            pltpu.VMEM((8, D, TOK), bf16),
            pltpu.VMEM((8, D, TOK), bf16),
            pltpu.VMEM((3, 8, TOK), f32),
            pltpu.VMEM((16, 8, TOK), f32),
            pltpu.VMEM((16, 8, TOK), f32),
            pltpu.VMEM((2, 8, TOK), f32),
            pltpu.VMEM((2, 8, TOK), f32),
            pltpu.VMEM((16, 8, TOK), f32),
            pltpu.VMEM((16, 8, TOK), f32),
            pltpu.VMEM((D, TOK), bf16),
            pltpu.VMEM((D, TOK), bf16),
        ] + [dma((n,)) for n in sems],
        compiler_params=pltpu.CompilerParams(
            collective_id=0, has_side_effects=True, vmem_limit_bytes=56 * 2 ** 20
        ),
        cost_estimate=pl.CostEstimate(flops=6 * 1024 * 1024 * D, bytes_accessed=2 ** 20, transcendentals=2 ** 20),
        name="contrastive",
    )(
        logit_scale.astype(f32).reshape(1),
        embeddings,
        jnp.broadcast_to(pair[None, :], (8, TOK)),
    )
    return emb_grad, loss, scale_grad


def solution(mesh):
    placed = (P("tower", "blk", None), P("blk"), P())
    return jax.shard_map(
        body,
        mesh=mesh,
        in_specs=placed,
        out_specs=(P("tower", "blk", None), P("tower"), P("tower")),
        check_vma=False,
    )
```

time: 1100 us -> 136 us (0.12)
  the two profiles are of different devices: /device:TPU:2 before, /device:TPU:5 now
where the time goes in v1:
time: 136 us
  Pallas kernels  128 us (94%)
  between operations  4.81 us (4%)
  local copies, waits for them, and re-layouts  2.89 us (2%)
    pallas_call x1, Pallas kernels, body(): pl.pallas_call(kernel, out_shape=(jax.ShapeDtypeStruct((1, TOK, D), bf16)...  128 us

profile of v1, /device:TPU:5, one launch (start us, length us, event | category | flops | bytes accessed | tf_op | source)
XLA Modules:
  0.0 135.6 jit_solution(4929850269513941858)
XLA Ops:
  1.3 0.0 copy-start
  1.3 0.6 copy-done
  1.9 0.6 broadcast_in_dim.2.pair_ref
  2.5 127.9 %contrastive.1 = (bf16[1,128,896]{2,1,0:T(8,128)(2,1)}, f32[1]{0:T(128)}, f32[1]{0:T(128)}) custom-call(f32[1]{0:T(128)} %bitcast.1.scale_ref, bf16[1,128,896]{2,1,0:T(8,128)(2,1)} %emb_ref.1, s32[8,128]{1,0:T(8,128)} %broadcast_in_dim.2.pair_ref), custom_call_target="tpu_custom_call" | custom-call | flops 5637144576 | bytes 1048576 | tf_op jit(solution)/shard_map/contrastive/pallas_call | solution.py:393
  130.5 1.6 %copy.10 = bf16[1,128,896]{2,1,0:T(8,128)(2,1)} copy(bf16[1,128,896]{2,1,0:T(8,128)(2,1)} %get-tuple-element.6) | data formatting | bytes 458752
Async XLA Ops:
  1.3 0.7 copy-start

commit v2 on v0

v2 whole, which is shorter than its diff:
```python
import jax
import jax.numpy as jnp
from jax import lax
from jax.experimental import pallas as pl
from jax.experimental.pallas import tpu as pltpu
from jax.sharding import PartitionSpec as P

eps = 1e-06
TOK = 128
D = 896
TOKENS = 16384
NY, NXH, NZ, NC = 4, 2, 8, 2
HALF, QUART = TOK // 2, TOK // 4
WIDE = 8 * TOK
f32 = jnp.float32
bf16 = jnp.bfloat16
MESH = pl.DeviceIdType.MESH
STEPS = 9
SENDS = 256


def device(t, y, xh, z, c):
    return (t, ((y * NXH + xh) * NZ + z) * NC + c)


def kernel(
    scale_ref, emb_ref, pair_ref,
    out_ref, loss_ref, sgrad_ref,
    own, images, texts, texts_t, pairs, exps, weights,
    text_part, text_send, ra_one, ra_two, ra_x, ra_fin, rb_odd, rb_even, rb_one, rb_two,
    image_part, image_send, image_sib, image_right, image_left,
    stat_send, z_img_all, z_txt_all, e_sums, scal_send, scal_z, scal_p, fin_send, fin_recv,
    s_all, r_txt, r_img, r_sib, r_pair, r_x, r_zi, r_zt, r_sz, r_sp,
    r_a1, r_a2, r_ax, r_af, r_bo, r_be, r_b1, r_b2, r_is, r_ir, r_il, r_fin,
):
    t = lax.axis_index("tower")
    b = lax.axis_index("blk")
    c = b % 2
    z = (b // 2) % 8
    xh = (b // 16) % 2
    y = b // 32
    odd = t == 1
    even = t == 0
    root = c == t
    line_rank = z * 2 + c
    plane_rank = (t * 4 + y) * 2 + xh
    me = y * 2 + xh
    scale = scale_ref[0]
    y_up, y_dn, y_far = (y + 1) % 4, (y + 3) % 4, (y + 2) % 4
    xo = 1 - xh

    conds = {
        "all": None, "odd": odd, "even": even, "root": root, "leaf": jnp.logical_not(root),
        "giver": jnp.logical_and(t == 0, c == 1), "taker": jnp.logical_and(t == 1, c == 1),
        "first": jnp.logical_and(t == 0, c == 0),
    }
    pending = {name: [] for name in conds}
    count = [0]

    def when(name):
        if name == "all":
            return lambda fn: fn()
        return pl.when(conds[name])

    def send(name, src, dst, rsem, target):
        slot = count[0]
        count[0] += 1
        ssem = s_all.at[slot]
        pltpu.make_async_remote_copy(
            src_ref=src, dst_ref=dst, send_sem=ssem, recv_sem=rsem,
            device_id=target, device_id_type=MESH,
        ).start()
        pending[name].append((slot, src.shape))

    def landed(dst, rsem):
        pltpu.make_async_copy(dst, dst, rsem).wait()

    up = device(t, y_up, xh, z, c)
    dn = device(t, y_dn, xh, z, c)
    zp = device(t, y, xh, (z + 1) % 8, c)
    zm = device(t, y, xh, (z + 7) % 8, c)
    sibling = device(t, y, xh, z, 1 - c)
    across = [device(1 - t, y, 0, z, c), device(1 - t, y, 1, z, c)]
    line_peers = [
        device(t, y, xh, (z + dz) % 8, (c + dc) % 2)
        for dz in (4, 3, 5, 2, 6, 1, 7, 0) for dc in (0, 1) if dz or dc
    ]
    plane_peers = [
        device((t + dt) % 2, (y + dy) % 4, (xh + dx) % 2, z, c)
        for dy in (2, 1, 3, 0) for dx in (1, 0) for dt in (0, 1) if dy or dx or dt
    ]
    line_others = [((z + dz) % 8) * 2 + (c + dc) % 2 for dz in range(8) for dc in range(2) if dz or dc]
    plane_others = [
        (((t + dt) % 2) * 4 + (y + dy) % 4) * 2 + (xh + dx) % 2
        for dy in range(4) for dx in range(2) for dt in range(2) if dy or dx or dt
    ]

    barrier = pltpu.get_barrier_semaphore()
    for peer in line_peers + plane_peers:
        pl.semaphore_signal(barrier, inc=1, device_id=peer, device_id_type=MESH)

    wide = emb_ref[0].astype(f32)
    lengths = jnp.sqrt(jnp.sum(wide * wide, axis=1, keepdims=True) + eps)
    unit = (wide / lengths).astype(bf16)

    @when("odd")
    def _():
        texts[me] = unit

    @when("giver")
    def _():
        own[...] = unit

    @when("first")
    def _():
        images[z] = unit

    @when("root")
    def _():
        pairs[z] = pair_ref[...]

    pl.semaphore_wait(barrier, 30)

    def rows(index, quarter, quarters):
        return texts.at[index, pl.ds(quarter * QUART, quarters * QUART)]

    def tsend(name, index, quarter, quarters, target):
        send(name, rows(index, quarter, quarters), rows(index, quarter, quarters), r_txt.at[index, quarter], target)

    def twait(index, quarter, quarters):
        landed(rows(index, quarter, quarters), r_txt.at[index, quarter])

    def ihalf(slot, h):
        return images.at[slot, pl.ds(h * HALF, HALF)]

    def isend(slot, h, target):
        send("root", ihalf(slot, h), ihalf(slot, h), r_img.at[slot, h], target)

    def iwait(slot, h):
        landed(ihalf(slot, h), r_img.at[slot, h])

    def to_sibling(slot):
        send("root", images.at[slot], images.at[slot], r_sib.at[slot], sibling)

    def image_hop(k):
        @when("root")
        def _():
            left, right = (z + 8 - k) % 8, (z + k) % 8
            for h in ((0, 1)):
                iwait(left, h)
                if k < 3 or h == 0:
                    isend(left, h, zp)
                iwait(right, h)
                if k < 3 or h == 1:
                    isend(right, h, zm)
            to_sibling(left)
            to_sibling(right)

    if STEPS > 1:
        @when("giver")
        def _():
            for h in range(2):
                part = own.at[pl.ds(h * HALF, HALF)]
                send("giver", part, ihalf(z, h), r_x.at[h], device(1, y, xh, z, c))

        @when("odd")
        def _():
            for e in range(2):
                tsend("odd", me, 0, 2, across[e])
            for peer in (up, dn):
                tsend("odd", me, 2, 2, peer)
            for e in range(2):
                tsend("odd", me, 2, 2, across[e])
            for peer in (up, dn):
                tsend("odd", me, 0, 2, peer)

        @when("root")
        def _():
            for h in range(2):
                @when("odd")
                def _():
                    landed(ihalf(z, h), r_x.at[h])
                isend(z, h, zp)
                isend(z, h, zm)
            to_sibling(z)
            for peer in line_peers:
                send("root", pair_ref, pairs.at[z], r_pair.at[z], peer)

        image_hop(1)

        @when("even")
        def _():
            for q in range(2):
                index = y * 2 + q
                twait(index, 0, 2)
                tsend("even", index, 0, 2, up)
                tsend("even", index, 0, 2, dn)
                tsend("even", index, xh, 1, across[1 - q])
            for q in range(2):
                index = y * 2 + q
                twait(index, 2, 2)
                tsend("even", index, 2 + xh, 1, across[1 - q])

        @when("odd")
        def _():
            index = y_dn * 2 + xh
            twait(index, 2, 2)
            tsend("odd", index, 2, 1, up)
            for e in range(2):
                tsend("odd", index, 2, 2, across[e])
            index = y_up * 2 + xh
            twait(index, 2, 2)
            tsend("odd", index, 3, 1, dn)
            for e in range(2):
                tsend("odd", index, 2, 2, across[e])

        image_hop(2)

        @when("odd")
        def _():
            for k in range(2):
                index = y * 2 + xo
                twait(index, k, 1)
                tsend("odd", index, k, 1, up)
                tsend("odd", index, k, 1, dn)
            for k in range(2):
                index = y_far * 2 + xh
                twait(index, 2 + k, 1)
                for e in range(2):
                    tsend("odd", index, 2 + k, 1, across[e])

        @when("even")
        def _():
            for ya in (y_dn, y_up):
                for q in range(2):
                    index = ya * 2 + q
                    twait(index, 2, 2)
                    tsend("even", index, 2 + xh, 1, across[1 - q])
            for q in range(2):
                index = y_dn * 2 + q
                twait(index, 0, 2)
                tsend("even", index, 0, 1, up)
                index = y_up * 2 + q
                twait(index, 0, 2)
                tsend("even", index, 1, 1, dn)

        image_hop(3)

        @when("odd")
        def _():
            index = y_dn * 2 + xh
            twait(index, 0, 2)
            tsend("odd", index, 0, 1, up)
            index = y_up * 2 + xh
            twait(index, 0, 2)
            tsend("odd", index, 1, 1, dn)
            index = y_dn * 2 + xo
            twait(index, 0, 1)
            tsend("odd", index, 0, 1, up)
            twait(index, 1, 1)
            index = y_up * 2 + xo
            twait(index, 1, 1)
            tsend("odd", index, 1, 1, dn)
            twait(index, 0, 1)
            for k in range(2):
                for q in range(2):
                    twait(y_far * 2 + q, k, 1)
            for ya in (y, y_dn, y_up, y_far):
                for k in range(2):
                    twait(ya * 2 + xo, 2 + k, 1)

        @when("even")
        def _():
            for q in range(2):
                index = y_far * 2 + q
                for k in range(2):
                    twait(index, 2 + k, 1)
                tsend("even", index, 2 + xh, 1, across[1 - q])
            for q in range(2):
                for k in range(2):
                    twait(y_far * 2 + q, k, 1)

        @when("root")
        def _():
            far = (z + 4) % 8
            for h in range(2):
                iwait(far, h)
            to_sibling(far)
            for dz in range(1, 8):
                landed(pairs.at[(z + dz) % 8], r_pair.at[(z + dz) % 8])

        @when("leaf")
        def _():
            for slot in range(8):
                landed(images.at[slot], r_sib.at[slot])
                landed(pairs.at[slot], r_pair.at[slot])

    def first_id(index):
        return ((index * 8 + z) * 2 + c) * TOK

    def pair_lanes():
        return jnp.concatenate([pairs[k][0:1] for k in range(8)], axis=1)

    sub_ids = lax.broadcasted_iota(jnp.int32, (TOK, 1), 0)

    def total(x):
        return jnp.sum(jnp.sum(x, axis=0, keepdims=True), axis=1, keepdims=True)

    if STEPS > 2:
        pair_row = pair_lanes()
        all_images = images[...].reshape(WIDE, D)

        def stats(p, carry):
            zi, ei, pi = carry
            two = texts[pl.ds(2 * p, 2)].reshape(2 * TOK, D)
            dots = lax.dot_general(two, all_images, (((1,), (1,)), ((), ())), preferred_element_type=f32)
            scores = scale * dots
            ex = jnp.exp(scores - scale)
            exps[pl.ds(2 * p, 2)] = ex.reshape(2, TOK, WIDE)
            es = ex * scores
            ids = jnp.concatenate([first_id(2 * p) + sub_ids, first_id(2 * p + 1) + sub_ids], axis=0)
            match = pair_row == ids
            zi = zi + jnp.sum(ex, axis=0, keepdims=True)
            ei = ei + jnp.sum(es, axis=0, keepdims=True)
            pi = pi + jnp.sum(jnp.where(match, scores, 0.0), axis=0, keepdims=True)
            zr = ex[:, 0:TOK]
            er = es[:, 0:TOK]
            for k in range(1, 8):
                zr = zr + ex[:, k * TOK:(k + 1) * TOK]
                er = er + es[:, k * TOK:(k + 1) * TOK]
            for h in range(2):
                part = slice(h * TOK, (h + 1) * TOK)
                stat_send[1, pl.ds(2 * p + h, 1), :] = jnp.sum(zr[part].T, axis=0, keepdims=True)
                e_sums[1, pl.ds(2 * p + h, 1), :] = jnp.sum(er[part].T, axis=0, keepdims=True)
            return zi, ei, pi

        zero = jnp.zeros((1, WIDE), f32)
        zi, ei, pi = lax.fori_loop(0, 4, stats, (zero, zero, zero))
        for k in range(8):
            stat_send[0, k:k + 1, :] = zi[:, k * TOK:(k + 1) * TOK]
            e_sums[0, k:k + 1, :] = ei[:, k * TOK:(k + 1) * TOK]

    if STEPS > 3:
        for peer in line_peers:
            send("all", stat_send.at[0], z_img_all.at[line_rank], r_zi.at[line_rank], peer)
        for peer in plane_peers:
            send("all", stat_send.at[1], z_txt_all.at[plane_rank], r_zt.at[plane_rank], peer)
        z_img_all[line_rank] = stat_send[0]
        z_txt_all[plane_rank] = stat_send[1]
        for k in range(8):
            texts_t[:, k * TOK:(k + 1) * TOK] = texts[k].astype(f32).T.astype(bf16)
        for other in line_others:
            landed(z_img_all.at[other], r_zi.at[other])
        for other in plane_others:
            landed(z_txt_all.at[other], r_zt.at[other])
        z_img = jnp.sum(z_img_all[...], axis=0)
        z_txt = jnp.sum(z_txt_all[...], axis=0)

    if STEPS > 4:
        half_img = 0.5 / z_img
        stat_send[2] = 0.5 / z_txt
        img_row = jnp.concatenate([half_img[k:k + 1] for k in range(8)], axis=1)

        def weigh(index, _):
            column = jnp.broadcast_to(stat_send[2, pl.ds(index, 1), :], (TOK, TOK)).T
            ids = first_id(index) + sub_ids
            for k in range(8):
                lanes = slice(k * TOK, (k + 1) * TOK)
                match = pair_row[:, lanes] == ids
                value = exps[index, :, lanes] * (img_row[:, lanes] + column)
                weights[index, :, lanes] = (value - jnp.where(match, 1.0, 0.0)).astype(bf16)
            return 0

        lax.fori_loop(0, 8, weigh, 0)

    def text_block(ya):
        pair_of = pl.ds(2 * ya, 2)
        two = weights[pair_of].reshape(2 * TOK, WIDE)
        part = jnp.dot(two, all_images, preferred_element_type=f32)
        text_part[pair_of] = part.reshape(2, TOK, D)

    def quart(ref, index, k):
        return ref.at[index, pl.ds(k * QUART, QUART)]

    def give_b(slot, ya):
        index = ya * 2 + xo
        text_send[index, HALF:TOK] = text_part[index, HALF:TOK].astype(bf16)
        for k in range(2):
            send("odd", quart(text_send, index, 2 + k), rb_even.at[slot, xh], r_be.at[slot, xh], across[k])

    def pass_b(slot, ya):
        for q in range(2):
            index = ya * 2 + q
            landed(rb_even.at[slot, 1 - q], r_be.at[slot, 1 - q])
            spot = pl.ds((2 + xh) * QUART, QUART)
            text_part[index, spot] = text_part[index, spot] + rb_even[slot, 1 - q].astype(f32)
            text_send[index, HALF:TOK] = text_part[index, HALF:TOK].astype(bf16)
            send("even", text_send.at[index, HALF:TOK], rb_odd.at[slot, xh], r_bo.at[slot, xh], across[q])

    def take_b(slot, ya):
        index = ya * 2 + xh
        for e in range(2):
            landed(rb_odd.at[slot, e], r_bo.at[slot, e])
        text_part[index, HALF:TOK] = (
            text_part[index, HALF:TOK] + rb_odd[slot, 0].astype(f32) + rb_odd[slot, 1].astype(f32)
        )

    def image_block(p):
        lanes = pl.ds(pl.multiple_of(p * 2 * TOK, 2 * TOK), 2 * TOK)
        part = jnp.dot(texts_t[...], weights[:, :, lanes].reshape(WIDE, 2 * TOK), preferred_element_type=f32)
        for h in range(2):
            image_part[2 * p + h] = part[:, h * TOK:(h + 1) * TOK]

        @when("leaf")
        def _():
            for h in range(2):
                image_send[2 * p + h] = part[:, h * TOK:(h + 1) * TOK].astype(bf16)
            both = pl.ds(2 * p, 2)
            send("leaf", image_send.at[both], image_sib.at[both], r_is.at[p], sibling)

    def add_sibling(p):
        both = pl.ds(2 * p, 2)
        landed(image_sib.at[both], r_is.at[p])
        for h in range(2):
            image_part[2 * p + h] = image_part[2 * p + h] + image_sib[2 * p + h].astype(f32)

    def dhalf(h):
        return pl.ds(h * (D // 2), D // 2)

    def ring_send(m, h, right):
        hops = 4 - m
        slot = (z + hops) % 8 if right else (z + 8 - hops) % 8
        into = image_right if right else image_left
        sem = r_ir if right else r_il
        spot = dhalf(h)
        value = image_part[slot, spot]
        if m > 1 or (m == 1 and h == (0 if right else 1)):
            landed(into.at[m - 1, spot], sem.at[m - 1, h])
            value = value + into[m - 1, spot].astype(f32)
        image_send[slot, spot] = value.astype(bf16)
        send("root", image_send.at[slot, spot], into.at[m, spot], sem.at[m, h], zp if right else zm)

    if STEPS > 5:
        text_block(y_far)
        for q in range(2):
            index = y_far * 2 + q
            text_send[index, 0:HALF] = text_part[index, 0:HALF].astype(bf16)
        far_two = pl.ds(2 * y_far, 2)
        send("all", text_send.at[far_two, 0:QUART], ra_one.at[0], r_a1.at[0], up)
        send("all", text_send.at[far_two, QUART:HALF], ra_one.at[1], r_a1.at[1], dn)
        orders = (y_far, y_dn, y_up, y)

        @when("odd")
        def _():
            give_b(0, y_far)

        for slot in (1, 2, 3):
            text_block(orders[slot])

            @when("odd")
            def _():
                give_b(slot, orders[slot])

        lane = lax.broadcasted_iota(jnp.int32, (8, TOK), 1)
        log_img = total(jnp.log(z_img))
        log_txt = total(jnp.log(z_txt))
        t_img = total(e_sums[0] / z_img)
        t_txt = total(e_sums[1] / z_txt)
        matched = jnp.sum(pi, axis=1, keepdims=True)
        scal_send[0] = jnp.where(
            lane == 0, log_txt,
            jnp.where(lane == 1, t_img, jnp.where(lane == 2, t_txt, jnp.where(lane == 3, matched, 0.0))),
        )
        for peer in line_peers:
            send("all", scal_send.at[0], scal_z.at[line_rank], r_sz.at[line_rank], peer)
        scal_z[line_rank] = scal_send[0]

        half_z = z // 2
        p_order = [(half_z + k) % 4 for k in (2, 1, 3, 0)]
        image_block(p_order[0])
        image_block(p_order[1])

        @when("even")
        def _():
            pass_b(0, y_far)

        def hop_a(way, ya, quarter, target):
            landed(ra_one.at[way], r_a1.at[way])
            for q in range(2):
                index = ya * 2 + q
                spot = slice(quarter * QUART, (quarter + 1) * QUART)
                text_part[index, spot] = text_part[index, spot] + ra_one[way, q].astype(f32)
                text_send[index, 0:HALF] = text_part[index, 0:HALF].astype(bf16)
            send("all", text_send.at[pl.ds(2 * ya, 2), 0:HALF], ra_two.at[way], r_a2.at[way], target)

        hop_a(0, y_up, 0, up)
        hop_a(1, y_dn, 1, dn)

        image_block(p_order[2])

        @when("even")
        def _():
            pass_b(1, y_dn)

        image_block(p_order[3])

        @when("root")
        def _():
            for p in p_order:
                add_sibling(p)
            ring_send(0, 0, True)
            ring_send(0, 1, False)
            ring_send(1, 1, True)
            ring_send(1, 0, False)

        @when("even")
        def _():
            pass_b(2, y_up)
            pass_b(3, y)

        @when("root")
        def _():
            ring_send(1, 0, True)
            ring_send(1, 1, False)

        @when("odd")
        def _():
            take_b(0, y_far)
            index = y_far * 2 + xh
            text_send[index, HALF:TOK] = text_part[index, HALF:TOK].astype(bf16)
            send("odd", quart(text_send, index, 2), rb_one.at[0], r_b1.at[0], up)
            send("odd", quart(text_send, index, 3), rb_one.at[1], r_b1.at[1], dn)

        @when("root")
        def _():
            for h in (1, 0):
                ring_send(2, h, True)
                ring_send(2, 1 - h, False)

        for way in range(2):
            landed(ra_two.at[way], r_a2.at[way])
        for q in range(2):
            index = y * 2 + q
            text_part[index, 0:HALF] = (
                text_part[index, 0:HALF] + ra_two[0, q].astype(f32) + ra_two[1, q].astype(f32)
            )

        @when("odd")
        def _():
            index = y * 2 + xo
            text_send[index, 0:HALF] = text_part[index, 0:HALF].astype(bf16)
            for k in range(2):
                send("odd", quart(text_send, index, k), ra_x.at[xh], r_ax.at[xh], across[k])

            take_b(1, y_dn)
            take_b(2, y_up)
            for way, ya, quarter, target in ((0, y_up, 2, up), (1, y_dn, 3, dn)):
                index = ya * 2 + xh
                landed(rb_one.at[way], r_b1.at[way])
                spot = slice(quarter * QUART, (quarter + 1) * QUART)
                text_part[index, spot] = text_part[index, spot] + rb_one[way].astype(f32)
                text_send[index, HALF:TOK] = text_part[index, HALF:TOK].astype(bf16)
                send("odd", text_send.at[index, HALF:TOK], rb_two.at[way], r_b2.at[way], target)

        @when("even")
        def _():
            for q in range(2):
                index = y * 2 + q
                landed(ra_x.at[1 - q], r_ax.at[1 - q])
                spot = pl.ds(xh * QUART, QUART)
                text_part[index, spot] = text_part[index, spot] + ra_x[1 - q].astype(f32)
                text_send[index, 0:HALF] = text_part[index, 0:HALF].astype(bf16)
                send("even", text_send.at[index, 0:HALF], ra_fin.at[xh], r_af.at[xh], across[q])

        @when("root")
        def _():
            for h in (1, 0):
                ring_send(3, h, True)
                ring_send(3, 1 - h, False)

        for other in line_others:
            landed(scal_z.at[other], r_sz.at[other])
        line_sum = jnp.sum(scal_z[...], axis=0)
        scal_send[1] = jnp.where(lane == 4, log_img, line_sum)
        for peer in plane_peers:
            send("all", scal_send.at[1], scal_p.at[plane_rank], r_sp.at[plane_rank], peer)
        scal_p[plane_rank] = scal_send[1]

        def finish(grads):
            unit32 = wide / lengths
            grads = scale * grads
            inner = jnp.sum(unit32 * grads, axis=1, keepdims=True)
            out_ref[0] = ((grads - unit32 * inner) / lengths).astype(bf16)

        @when("root")
        def _():
            for h in range(2):
                landed(image_right.at[3, dhalf(h)], r_ir.at[3, h])
                landed(image_left.at[3, dhalf(h)], r_il.at[3, h])
            acc = image_part[z] + image_right[3].astype(f32) + image_left[3].astype(f32)

            @when("odd")
            def _():
                fin_send[...] = acc.astype(bf16)
                send("taker", fin_send, fin_recv, r_fin.at[0], device(0, y, xh, z, c))

            @when("even")
            def _():
                finish(acc.T)

        @when("odd")
        def _():
            take_b(3, y)
            for way in range(2):
                landed(rb_two.at[way], r_b2.at[way])
            text_part[me, HALF:TOK] = (
                text_part[me, HALF:TOK] + rb_two[0].astype(f32) + rb_two[1].astype(f32)
            )
            for e in range(2):
                landed(ra_fin.at[e], r_af.at[e])
            text_part[me, 0:HALF] = (
                text_part[me, 0:HALF] + ra_fin[0].astype(f32) + ra_fin[1].astype(f32)
            )
            finish(text_part[me])

        @when("giver")
        def _():
            landed(fin_recv, r_fin.at[0])
            finish(fin_recv[...].astype(f32).T)

        for other in plane_others:
            landed(scal_p.at[other], r_sp.at[other])
        all_sum = jnp.sum(scal_p[...], axis=0)

        def pick(x, k):
            return jnp.sum(jnp.where(lane[0:1] == k, x[0:1], 0.0))

        log_all = jnp.where(odd, pick(line_sum, 0), pick(all_sum, 4))
        t_all = jnp.where(odd, pick(all_sum, 2), pick(all_sum, 1))
        p_all = pick(all_sum, 3)
        loss_ref[0] = (scale * TOKENS + log_all - p_all) * (1.0 / (2 * TOKENS))
        sgrad_ref[0] = (t_all - p_all) / scale * (1.0 / (2 * TOKENS))

    sizes = {
        (QUART, D): texts.at[0, 0:QUART], (HALF, D): texts.at[0, 0:HALF], (TOK, D): texts.at[0],
        (2, QUART, D): texts.at[0:2, 0:QUART], (2, HALF, D): texts.at[0:2, 0:HALF],
        (8, TOK): stat_send.at[0], (2, D, TOK): image_send.at[0:2],
        (D // 2, TOK): image_send.at[0, 0:D // 2], (D, TOK): fin_send,
    }
    for name, copies in pending.items():
        if copies:
            @when(name)
            def _():
                for slot, shape in copies:
                    pltpu.make_async_copy(sizes[shape], sizes[shape], s_all.at[slot]).wait()


def body(embeddings, pair, logit_scale):
    vmem = pl.BlockSpec(memory_space=pltpu.VMEM)
    smem = pl.BlockSpec(memory_space=pltpu.SMEM)
    dma = pltpu.SemaphoreType.DMA
    scratch = [
        ((TOK, D), bf16),
        ((8, TOK, D), bf16),
        ((8, TOK, D), bf16),
        ((D, WIDE), bf16),
        ((8, 8, TOK), jnp.int32),
        ((8, TOK, WIDE), f32),
        ((8, TOK, WIDE), bf16),
        ((8, TOK, D), f32),
        ((8, TOK, D), bf16),
        ((2, 2, QUART, D), bf16),
        ((2, 2, HALF, D), bf16),
        ((2, QUART, D), bf16),
        ((2, HALF, D), bf16),
        ((4, 2, HALF, D), bf16),
        ((4, 2, QUART, D), bf16),
        ((2, QUART, D), bf16),
        ((2, HALF, D), bf16),
        ((8, D, TOK), f32),
        ((8, D, TOK), bf16),
        ((8, D, TOK), bf16),
        ((4, D, TOK), bf16),
        ((4, D, TOK), bf16),
        ((3, 8, TOK), f32),
        ((16, 8, TOK), f32),
        ((16, 8, TOK), f32),
        ((2, 8, TOK), f32),
        ((2, 8, TOK), f32),
        ((16, 8, TOK), f32),
        ((16, 8, TOK), f32),
        ((D, TOK), bf16),
        ((D, TOK), bf16),
    ]
    sems = [
        (SENDS,), (8, 4), (8, 2), (8,), (8,), (2,), (16,), (16,), (16,), (16,),
        (2,), (2,), (2,), (2,), (4, 2), (4, 2), (2,), (2,), (4,), (4, 2), (4, 2), (1,),
    ]
    return pl.pallas_call(
        kernel,
        out_shape=(
            jax.ShapeDtypeStruct((1, TOK, D), bf16),
            jax.ShapeDtypeStruct((1,), f32),
            jax.ShapeDtypeStruct((1,), f32),
        ),
        in_specs=[smem, vmem, vmem],
        out_specs=(vmem, smem, smem),
        scratch_shapes=[pltpu.VMEM(shape, dtype) for shape, dtype in scratch] + [dma(shape) for shape in sems],
        compiler_params=pltpu.CompilerParams(
            collective_id=0, has_side_effects=True, vmem_limit_bytes=56 * 2 ** 20
        ),
        cost_estimate=pl.CostEstimate(flops=6 * WIDE * WIDE * D, bytes_accessed=2 ** 20, transcendentals=2 ** 20),
        name="contrastive",
    )(
        logit_scale.astype(f32).reshape(1),
        embeddings,
        jnp.broadcast_to(pair[None, :], (8, TOK)),
    )


def solution(mesh):
    placed = (P("tower", "blk", None), P("blk"), P())
    return jax.shard_map(
        body,
        mesh=mesh,
        in_specs=placed,
        out_specs=(P("tower", "blk", None), P("tower"), P("tower")),
        check_vma=False,
    )
```

time: 1100 us -> 82.4 us (0.07)
  the two profiles are of different devices: /device:TPU:2 before, /device:TPU:1 now
where the time goes in v2:
time: 82.4 us; the launch traced here: 82.3 us
  Pallas kernels  74.6 us (91%)
  between operations  4.81 us (6%)
  local copies, waits for them, and re-layouts  2.89 us (4%)
    pallas_call x1, Pallas kernels, body(): pl.pallas_call(kernel, out_shape=(jax.ShapeDtypeStruct((1, TOK, D), bf16)...  74.6 us
    unnamed x3, local copies, waits for them, and re-layouts  2.29 us

profile of v2, /device:TPU:1, one launch (start us, length us, event | category | flops | bytes accessed | tf_op | source)
XLA Modules:
  0.0 82.3 jit_solution(15752607694773988531)
XLA Ops:
  1.3 0.0 copy-start
  1.3 0.6 copy-done
  1.9 0.6 broadcast_in_dim.2.pair_ref
  2.5 74.6 %contrastive.1 = (bf16[1,128,896]{2,1,0:T(8,128)(2,1)}, f32[1]{0:T(128)}, f32[1]{0:T(128)}) custom-call(f32[1]{0:T(128)} %bitcast.1.scale_ref, bf16[1,128,896]{2,1,0:T(8,128)(2,1)} %emb_ref.1, s32[8,128]{1,0:T(8,128)} %broadcast_in_dim.2.pair_ref), custom_call_target="tpu_custom_call" | custom-call | flops 5637144576 | bytes 1048576 | tf_op jit(solution)/shard_map/contrastive/pallas_call | solution.py:699
  77.1 1.6 %copy.10 = bf16[1,128,896]{2,1,0:T(8,128)(2,1)} copy(bf16[1,128,896]{2,1,0:T(8,128)(2,1)} %get-tuple-element.6) | data formatting | bytes 458752
Async XLA Ops:
  1.3 0.7 copy-start

commit v3 on v2

v3 whole, which is shorter than its diff:
```python
import jax
import jax.numpy as jnp
from jax import lax
from jax.experimental import pallas as pl
from jax.experimental.pallas import tpu as pltpu
from jax.sharding import PartitionSpec as P

eps = 1e-06
TOK = 128
D = 896
TOKENS = 16384
NY, NXH, NZ, NC = 4, 2, 8, 2
HALF, QUART = TOK // 2, TOK // 4
WIDE = 8 * TOK
f32 = jnp.float32
bf16 = jnp.bfloat16
MESH = pl.DeviceIdType.MESH
STEPS = 9
SENDS = 320


def device(t, y, xh, z, c):
    return (t, ((y * NXH + xh) * NZ + z) * NC + c)


def kernel(
    scale_ref, emb_hbm, pair_ref,
    out_ref, loss_ref, sgrad_ref,
    emb_ref, own, images, texts, pairs, exps, weights,
    text_part, text_send, ra_one, ra_two, ra_x, ra_fin, rb_odd, rb_even, rb_one, rb_two,
    image_part, image_send, image_sib, image_right, image_left,
    stat_send, z_img_all, z_txt_all, e_sums, scal_send, scal_z, scal_p, fin_send, fin_recv,
    s_in, s_all, r_txt, r_img, r_sib, r_pair, r_x, r_zi, r_zt, r_sz, r_sp,
    r_a1, r_a2, r_ax, r_af, r_bo, r_be, r_b1, r_b2, r_is, r_ir, r_il, r_fin,
):
    t = lax.axis_index("tower")
    b = lax.axis_index("blk")
    c = b % 2
    z = (b // 2) % 8
    xh = (b // 16) % 2
    y = b // 32
    odd = t == 1
    even = t == 0
    line_rank = z * 2 + c
    plane_rank = (t * 4 + y) * 2 + xh
    me = y * 2 + xh
    scale = scale_ref[0]
    y_up, y_dn, y_far = (y + 1) % 4, (y + 3) % 4, (y + 2) % 4
    xo = 1 - xh

    conds = {"all": None, "odd": odd, "even": even}
    pending = {name: [] for name in conds}
    count = [0]

    def when(name):
        if name == "all":
            return lambda fn: fn()
        return pl.when(conds[name])

    def send(name, src, dst, rsem, target):
        slot = count[0]
        count[0] += 1
        pltpu.make_async_remote_copy(
            src_ref=src, dst_ref=dst, send_sem=s_all.at[slot], recv_sem=rsem,
            device_id=target, device_id_type=MESH,
        ).start()
        pending[name].append((slot, src.shape))

    def landed(dst, rsem):
        pltpu.make_async_copy(dst, dst, rsem).wait()

    up = device(t, y_up, xh, z, c)
    dn = device(t, y_dn, xh, z, c)
    zp = device(t, y, xh, (z + 1) % 8, c)
    zm = device(t, y, xh, (z + 7) % 8, c)
    sibling = device(t, y, xh, z, 1 - c)
    across = [device(1 - t, y, 0, z, c), device(1 - t, y, 1, z, c)]
    partner = device(1 - t, y, xh, z, c)
    line_peers = [
        device(t, y, xh, (z + dz) % 8, (c + dc) % 2)
        for dz in (4, 3, 5, 2, 6, 1, 7, 0) for dc in (0, 1) if dz or dc
    ]
    plane_peers = [
        device((t + dt) % 2, (y + dy) % 4, (xh + dx) % 2, z, c)
        for dy in (2, 1, 3, 0) for dx in (1, 0) for dt in (0, 1) if dy or dx or dt
    ]
    line_others = [((z + dz) % 8) * 2 + (c + dc) % 2 for dz in range(8) for dc in range(2) if dz or dc]
    plane_others = [
        (((t + dt) % 2) * 4 + (y + dy) % 4) * 2 + (xh + dx) % 2
        for dy in range(4) for dx in range(2) for dt in range(2) if dy or dx or dt
    ]

    fetch = pltpu.make_async_copy(emb_hbm.at[0], emb_ref, s_in.at[0])
    fetch.start()
    barrier = pltpu.get_barrier_semaphore()
    for peer in (up, dn, zp, zm, sibling, across[0], across[1]):
        pl.semaphore_signal(barrier, inc=1, device_id=peer, device_id_type=MESH)
    fetch.wait()

    def normal(part):
        wide = emb_ref[part].astype(f32)
        lengths = jnp.sqrt(jnp.sum(wide * wide, axis=1, keepdims=True) + eps)
        return wide / lengths, lengths

    lower, upper = slice(0, HALF), slice(HALF, TOK)
    unit_low = normal(lower)[0].astype(bf16)
    unit_high = normal(upper)[0].astype(bf16)

    @when("odd")
    def _():
        texts[me, lower] = unit_low
        texts[me, upper] = unit_high

    @when("even")
    def _():
        images[z, c] = unit_low
        own[...] = unit_high

    pairs[z, c] = jnp.broadcast_to(pair_ref[...], (8, TOK))
    pl.semaphore_wait(barrier, 7)

    def rows(index, quarter, quarters):
        return texts.at[index, pl.ds(quarter * QUART, quarters * QUART)]

    def tsend(name, index, quarter, quarters, target):
        send(name, rows(index, quarter, quarters), rows(index, quarter, quarters), r_txt.at[index, quarter], target)

    def twait(index, quarter, quarters):
        landed(rows(index, quarter, quarters), r_txt.at[index, quarter])

    def piece(slot, h):
        return images.at[slot, c, pl.ds(h * QUART, QUART)]

    def isend(name, slot, h, target):
        send(name, piece(slot, h), piece(slot, h), r_img.at[slot, h], target)

    def iwait(slot, h):
        landed(piece(slot, h), r_img.at[slot, h])

    def to_sibling(name, slot):
        send(name, images.at[slot, c], images.at[slot, c], r_sib.at[slot], sibling)

    def image_hop(name, k, h):
        left, right = (z + 8 - k) % 8, (z + k) % 8
        iwait(left, h)
        if k < 3 or h == 0:
            isend(name, left, h, zp)
        iwait(right, h)
        if k < 3 or h == 1:
            isend(name, right, h, zm)
        if h == 1:
            to_sibling(name, left)
            to_sibling(name, right)

    def image_last(name):
        far = (z + 4) % 8
        for h in range(2):
            iwait(far, h)
        to_sibling(name, far)
        for slot in range(8):
            landed(images.at[slot, 1 - c], r_sib.at[slot])

    if STEPS > 1:
        @when("even")
        def _():
            n = "even"
            for h in range(2):
                isend(n, z, h, zp)
                isend(n, z, h, zm)
                send(n, own.at[pl.ds(h * QUART, QUART)], piece(z, h), r_x.at[h], partner)
            to_sibling(n, z)
            image_hop(n, 1, 0)
            for q in range(2):
                index = y * 2 + q
                twait(index, 0, 2)
                tsend(n, index, xh, 1, across[1 - q])
                tsend(n, index, 0, 2, up)
                tsend(n, index, 0, 2, dn)
            image_hop(n, 1, 1)
            for q in range(2):
                index = y * 2 + q
                twait(index, 2 + xh, 1)
                tsend(n, index, 2 + xh, 1, across[1 - q])
            image_hop(n, 2, 0)
            for q in range(2):
                index = y_dn * 2 + q
                twait(index, 2 + xh, 1)
                tsend(n, index, 2 + xh, 1, across[1 - q])
            image_hop(n, 2, 1)
            for q in range(2):
                index = y_up * 2 + q
                twait(index, 2 + xh, 1)
                tsend(n, index, 2 + xh, 1, across[1 - q])
            for q in range(2):
                index = y_dn * 2 + q
                twait(index, 0, 2)
                tsend(n, index, 0, 1, up)
                index = y_up * 2 + q
                twait(index, 0, 2)
                tsend(n, index, 1, 1, dn)
                if q == 0:
                    image_hop(n, 3, 0)
            image_hop(n, 3, 1)
            for q in range(2):
                index = y_far * 2 + q
                twait(index, 2 + xh, 1)
                tsend(n, index, 2 + xh, 1, across[1 - q])
            image_last(n)
            for ya in (y, y_dn, y_up, y_far):
                for q in range(2):
                    twait(ya * 2 + q, 2 + xo, 1)
            for q in range(2):
                for k in range(2):
                    twait(y_far * 2 + q, k, 1)

        @when("odd")
        def _():
            n = "odd"
            mine, below, above, far = me, y_dn * 2 + xh, y_up * 2 + xh, y_far * 2 + xh
            for e in range(2):
                tsend(n, mine, 0, 2, across[e])
            for peer in (up, dn):
                tsend(n, mine, 2, 2, peer)
            for e in range(2):
                tsend(n, mine, 2 + e, 1, across[e])
            for peer in (up, dn):
                tsend(n, mine, 0, 2, peer)
            for h in range(2):
                landed(piece(z, h), r_x.at[h])
                isend(n, z, h, zp)
                isend(n, z, h, zm)
            to_sibling(n, z)
            twait(below, 2, 2)
            tsend(n, below, 2, 1, up)
            for e in range(2):
                tsend(n, below, 2 + e, 1, across[e])
            twait(above, 2, 2)
            tsend(n, above, 3, 1, dn)
            for e in range(2):
                tsend(n, above, 2 + e, 1, across[e])
            image_hop(n, 1, 0)
            twait(below, 0, 2)
            tsend(n, below, 0, 1, up)
            twait(above, 0, 2)
            tsend(n, above, 1, 1, dn)
            image_hop(n, 1, 1)
            for k in range(2):
                index = y * 2 + xo
                twait(index, k, 1)
                tsend(n, index, k, 1, up)
                tsend(n, index, k, 1, dn)
            for k in range(2):
                twait(far, 2 + k, 1)
                tsend(n, far, 2 + k, 1, across[k])
            for e in range(2):
                tsend(n, mine, 3 - e, 1, across[e])
                tsend(n, below, 3 - e, 1, across[e])
            image_hop(n, 2, 0)
            for e in range(2):
                tsend(n, above, 3 - e, 1, across[e])
                tsend(n, far, 3 - e, 1, across[e])
            image_hop(n, 2, 1)
            index = y_dn * 2 + xo
            twait(index, 0, 1)
            tsend(n, index, 0, 1, up)
            index = y_up * 2 + xo
            twait(index, 1, 1)
            tsend(n, index, 1, 1, dn)
            image_hop(n, 3, 0)
            image_hop(n, 3, 1)
            image_last(n)
            twait(y_dn * 2 + xo, 1, 1)
            twait(y_up * 2 + xo, 0, 1)
            for k in range(2):
                for q in range(2):
                    twait(y_far * 2 + q, k, 1)
            for ya in (y, y_dn, y_up, y_far):
                for k in range(2):
                    twait(ya * 2 + xo, 2 + k, 1)

        for peer in line_peers:
            send("all", pairs.at[z, c], pairs.at[z, c], r_pair.at[line_rank], peer)

    def first_id(index):
        return ((index * 8 + z) * 2 + c) * TOK

    sub_ids = lax.broadcasted_iota(jnp.int32, (TOK, 1), 0)

    def total(x):
        return jnp.sum(jnp.sum(x, axis=0, keepdims=True), axis=1, keepdims=True)

    if STEPS > 2:
        all_images = images[...].reshape(WIDE, D)

        def stats(p, carry):
            zi, ei = carry
            two = texts[pl.ds(2 * p, 2)].reshape(2 * TOK, D)
            dots = lax.dot_general(two, all_images, (((1,), (1,)), ((), ())), preferred_element_type=f32)
            scores = scale * dots
            ex = jnp.exp(scores - scale)
            exps[pl.ds(2 * p, 2)] = ex.reshape(2, TOK, WIDE)
            es = ex * scores
            zi = zi + jnp.sum(ex, axis=0, keepdims=True)
            ei = ei + jnp.sum(es, axis=0, keepdims=True)
            zr = ex[:, 0:TOK]
            er = es[:, 0:TOK]
            for k in range(1, 8):
                zr = zr + ex[:, k * TOK:(k + 1) * TOK]
                er = er + es[:, k * TOK:(k + 1) * TOK]
            for h in range(2):
                part = slice(h * TOK, (h + 1) * TOK)
                stat_send[1, pl.ds(2 * p + h, 1), :] = jnp.sum(zr[part].T, axis=0, keepdims=True)
                e_sums[1, pl.ds(2 * p + h, 1), :] = jnp.sum(er[part].T, axis=0, keepdims=True)
            return zi, ei

        zero = jnp.zeros((1, WIDE), f32)
        zi, ei = lax.fori_loop(0, 4, stats, (zero, zero))
        for k in range(8):
            stat_send[0, k:k + 1, :] = zi[:, k * TOK:(k + 1) * TOK]
            e_sums[0, k:k + 1, :] = ei[:, k * TOK:(k + 1) * TOK]

    if STEPS > 3:
        for peer in line_peers:
            send("all", stat_send.at[0], z_img_all.at[line_rank], r_zi.at[line_rank], peer)
        for peer in plane_peers:
            send("all", stat_send.at[1], z_txt_all.at[plane_rank], r_zt.at[plane_rank], peer)
        z_img_all[line_rank] = stat_send[0]
        z_txt_all[plane_rank] = stat_send[1]
        for dz in range(8):
            for dc in range(2):
                if dz or dc:
                    zo, co = (z + dz) % 8, (c + dc) % 2
                    landed(pairs.at[zo, co], r_pair.at[zo * 2 + co])

        def own_half(k, core):
            line = pairs[k, core, 0:1]
            return jnp.where(odd, line[:, HALF:TOK], line[:, 0:HALF])

        pair_row = jnp.concatenate([own_half(k, core) for k in range(8) for core in range(2)], axis=1)
        for other in line_others:
            landed(z_img_all.at[other], r_zi.at[other])
        for other in plane_others:
            landed(z_txt_all.at[other], r_zt.at[other])
        z_img = jnp.sum(z_img_all[...], axis=0)
        z_txt = jnp.sum(z_txt_all[...], axis=0)

    if STEPS > 4:
        half_img = 0.5 / z_img
        stat_send[2] = 0.5 / z_txt
        img_row = jnp.concatenate([half_img[k:k + 1] for k in range(8)], axis=1)

        def weigh(index, carry):
            column = jnp.broadcast_to(stat_send[2, pl.ds(index, 1), :], (TOK, TOK)).T
            ids = first_id(index) + sub_ids
            hits = []
            for k in range(8):
                lanes = slice(k * TOK, (k + 1) * TOK)
                match = pair_row[:, lanes] == ids
                ex = exps[index, :, lanes]
                value = ex * (img_row[:, lanes] + column)
                weights[index, :, lanes] = (value - jnp.where(match, 1.0, 0.0)).astype(bf16)
                hits.append(jnp.sum(jnp.where(match, ex, 0.0), axis=0, keepdims=True))
            return carry + jnp.concatenate(hits, axis=1)

        hit = lax.fori_loop(0, 8, weigh, jnp.zeros((1, WIDE), f32))

    def text_block(ya):
        pair_of = pl.ds(2 * ya, 2)
        two = weights[pair_of].reshape(2 * TOK, WIDE)
        part = jnp.dot(two, all_images, preferred_element_type=f32)
        text_part[pair_of] = part.reshape(2, TOK, D)

    def quart(k):
        return pl.ds(k * QUART, QUART)

    def stage(index, k):
        text_send[index, quart(k)] = text_part[index, quart(k)].astype(bf16)
        return text_send.at[index, quart(k)]

    def stage_two(ya, k):
        for q in range(2):
            stage(ya * 2 + q, k)
        return text_send.at[pl.ds(2 * ya, 2), quart(k)]

    def add(index, k, value):
        text_part[index, quart(k)] = text_part[index, quart(k)] + value.astype(f32)

    def give_b(slot, ya):
        for k in range(2):
            send("odd", stage(ya * 2 + xo, 2 + k), rb_even.at[slot, xh], r_be.at[slot, xh], across[k])

    def free_b(slot, ya):
        for q in range(2):
            send("even", stage(ya * 2 + q, 2 + xo), rb_odd.at[slot, xh, 0], r_bo.at[slot, xh, 0], across[q])

    def pass_b(slot, ya):
        for q in range(2):
            index = ya * 2 + q
            landed(rb_even.at[slot, 1 - q], r_be.at[slot, 1 - q])
            add(index, 2 + xh, rb_even[slot, 1 - q])
            send("even", stage(index, 2 + xh), rb_odd.at[slot, xh, 1], r_bo.at[slot, xh, 1], across[q])

    def take_b(slot, ya):
        index = ya * 2 + xh
        for part in range(2):
            for e in range(2):
                landed(rb_odd.at[slot, e, part], r_bo.at[slot, e, part])
                add(index, 2 + (e if part else 1 - e), rb_odd[slot, e, part])

    def image_block(p):
        lanes = pl.ds(pl.multiple_of(p * 2 * TOK, 2 * TOK), 2 * TOK)
        part = lax.dot_general(
            weights[:, :, lanes].reshape(WIDE, 2 * TOK), texts[...].reshape(WIDE, D),
            (((0,), (0,)), ((), ())), preferred_element_type=f32,
        )
        both = pl.ds(2 * p, 2)
        image_part[both] = part.reshape(2, 2, HALF, D)
        image_send[both, 1 - c] = image_part[both, 1 - c].astype(bf16)
        send("all", image_send.at[both, 1 - c], image_sib.at[both], r_is.at[p], sibling)

    def add_sibling(p):
        both = pl.ds(2 * p, 2)
        landed(image_sib.at[both], r_is.at[p])
        image_part[both, c] = image_part[both, c] + image_sib[both].astype(f32)

    def ring_send(m, h, right):
        hops = 4 - m
        slot = (z + hops) % 8 if right else (z + 8 - hops) % 8
        into = image_right if right else image_left
        sem = r_ir if right else r_il
        value = image_part[slot, c, quart(h)]
        if m > 1 or (m == 1 and h == (0 if right else 1)):
            landed(into.at[m - 1, quart(h)], sem.at[m - 1, h])
            value = value + into[m - 1, quart(h)].astype(f32)
        image_send[slot, c, quart(h)] = value.astype(bf16)
        send(
            "all", image_send.at[slot, c, quart(h)], into.at[m, quart(h)], sem.at[m, h], zp if right else zm
        )

    if STEPS > 5:
        half_z = z // 2
        p_far, p_up, p_dn, p_own = [(half_z + k) % 4 for k in (2, 1, 3, 0)]

        image_block(p_far)
        text_block(y_far)
        send("all", stage_two(y_far, 0), ra_one.at[0], r_a1.at[0], up)
        send("all", stage_two(y_far, 1), ra_one.at[1], r_a1.at[1], dn)

        def spread(slot, ya):
            @when("odd")
            def _():
                give_b(slot, ya)

            @when("even")
            def _():
                free_b(slot, ya)

        spread(0, y_far)
        text_block(y_dn)
        send("all", stage_two(y_dn, 0), ra_two.at[1, 0], r_a2.at[1, 0], dn)
        spread(1, y_dn)
        add_sibling(p_far)
        ring_send(0, 0, True)
        ring_send(0, 1, False)
        text_block(y_up)
        send("all", stage_two(y_up, 1), ra_two.at[0, 0], r_a2.at[0, 0], up)
        spread(2, y_up)
        image_block(p_up)

        @when("even")
        def _():
            pass_b(0, y_far)

        image_block(p_dn)
        add_sibling(p_up)

        def hop_a(way, ya, target):
            landed(ra_one.at[way], r_a1.at[way])
            for q in range(2):
                add(ya * 2 + q, way, ra_one[way, q])
            send("all", stage_two(ya, way), ra_two.at[way, 1], r_a2.at[way, 1], target)

        hop_a(0, y_up, up)
        hop_a(1, y_dn, dn)
        add_sibling(p_dn)
        ring_send(1, 1, True)
        ring_send(1, 0, False)
        text_block(y)
        spread(3, y)

        @when("even")
        def _():
            pass_b(1, y_dn)

        ring_send(1, 0, True)
        ring_send(1, 1, False)
        image_block(p_own)

        @when("even")
        def _():
            pass_b(2, y_up)
            pass_b(3, y)

        lane = lax.broadcasted_iota(jnp.int32, (8, TOK), 1)
        log_img = total(jnp.log(z_img))
        log_txt = total(jnp.log(z_txt))
        t_img = total(e_sums[0] / z_img)
        t_txt = total(e_sums[1] / z_txt)
        found = hit > 0.0
        matched = jnp.sum(
            jnp.where(found, jnp.log(jnp.where(found, hit, 1.0)) + scale, 0.0), axis=1, keepdims=True
        )
        scal_send[0] = jnp.where(
            lane == 0, log_txt,
            jnp.where(lane == 1, t_img, jnp.where(lane == 2, t_txt, jnp.where(lane == 3, matched, 0.0))),
        )
        for peer in line_peers:
            send("all", scal_send.at[0], scal_z.at[line_rank], r_sz.at[line_rank], peer)
        scal_z[line_rank] = scal_send[0]
        add_sibling(p_own)

        @when("odd")
        def _():
            take_b(0, y_far)
            send("odd", stage(y_far * 2 + xh, 2), rb_one.at[0], r_b1.at[0], up)
            send("odd", stage(y_far * 2 + xh, 3), rb_one.at[1], r_b1.at[1], dn)

        for h in (1, 0):
            ring_send(2, h, True)
            ring_send(2, 1 - h, False)

        for part in range(2):
            for way in range(2):
                landed(ra_two.at[way, part], r_a2.at[way, part])
                for q in range(2):
                    add(y * 2 + q, way if part else 1 - way, ra_two[way, part, q])

        @when("odd")
        def _():
            for k in range(2):
                send("odd", stage(y * 2 + xo, k), ra_x.at[xh], r_ax.at[xh], across[k])
            take_b(1, y_dn)
            take_b(2, y_up)
            send("odd", stage(y_up * 2 + xh, 3), rb_two.at[0, 0], r_b2.at[0, 0], up)
            send("odd", stage(y_dn * 2 + xh, 2), rb_two.at[1, 0], r_b2.at[1, 0], dn)
            for way, ya, target in ((0, y_up, up), (1, y_dn, dn)):
                landed(rb_one.at[way], r_b1.at[way])
                add(ya * 2 + xh, 2 + way, rb_one[way])
                send("odd", stage(ya * 2 + xh, 2 + way), rb_two.at[way, 1], r_b2.at[way, 1], target)

        @when("even")
        def _():
            for q in range(2):
                send("even", stage(y * 2 + q, xo), ra_fin.at[xh, 0], r_af.at[xh, 0], across[q])

        for h in (1, 0):
            ring_send(3, h, True)
            ring_send(3, 1 - h, False)

        @when("even")
        def _():
            for q in range(2):
                landed(ra_x.at[1 - q], r_ax.at[1 - q])
                add(y * 2 + q, xh, ra_x[1 - q])
                send("even", stage(y * 2 + q, xh), ra_fin.at[xh, 1], r_af.at[xh, 1], across[q])

        for other in line_others:
            landed(scal_z.at[other], r_sz.at[other])
        line_sum = jnp.sum(scal_z[...], axis=0)
        scal_send[1] = jnp.where(lane == 4, log_img, line_sum)
        for peer in plane_peers:
            send("all", scal_send.at[1], scal_p.at[plane_rank], r_sp.at[plane_rank], peer)
        scal_p[plane_rank] = scal_send[1]

        def finish(part, grads):
            unit32, lengths = normal(part)
            grads = scale * grads
            inner = jnp.sum(unit32 * grads, axis=1, keepdims=True)
            out_ref[0, part] = ((grads - unit32 * inner) / lengths).astype(bf16)

        @when("odd")
        def _():
            take_b(3, y)

        for h in range(2):
            landed(image_right.at[3, quart(h)], r_ir.at[3, h])
            landed(image_left.at[3, quart(h)], r_il.at[3, h])
        acc = image_part[z, c] + image_right[3].astype(f32) + image_left[3].astype(f32)

        @when("odd")
        def _():
            fin_send[...] = acc.astype(bf16)
            send("odd", fin_send, fin_recv, r_fin.at[0], partner)
            for part in range(2):
                for way in range(2):
                    landed(rb_two.at[way, part], r_b2.at[way, part])
                    add(me, 2 + (way if part else 1 - way), rb_two[way, part])
            finish(upper, text_part[me, upper])
            for part in range(2):
                for e in range(2):
                    landed(ra_fin.at[e, part], r_af.at[e, part])
                    add(me, e if part else 1 - e, ra_fin[e, part])
            finish(lower, text_part[me, lower])

        @when("even")
        def _():
            finish(lower, acc)
            landed(fin_recv, r_fin.at[0])
            finish(upper, fin_recv[...].astype(f32))

        for other in plane_others:
            landed(scal_p.at[other], r_sp.at[other])
        all_sum = jnp.sum(scal_p[...], axis=0)

        def pick(x, k):
            return jnp.sum(jnp.where(lane[0:1] == k, x[0:1], 0.0))

        log_all = jnp.where(odd, pick(line_sum, 0), pick(all_sum, 4))
        t_all = jnp.where(odd, pick(all_sum, 2), pick(all_sum, 1))
        p_all = pick(all_sum, 3)
        loss_ref[0] = (scale * TOKENS + log_all - p_all) * (1.0 / (2 * TOKENS))
        sgrad_ref[0] = (t_all - p_all) / scale * (1.0 / (2 * TOKENS))

    sizes = {
        (QUART, D): texts.at[0, 0:QUART], (HALF, D): texts.at[0, 0:HALF],
        (2, QUART, D): texts.at[0:2, 0:QUART], (2, HALF, D): texts.at[0:2, 0:HALF],
        (8, TOK): stat_send.at[0],
    }
    for name, copies in pending.items():
        if copies:
            @when(name)
            def _():
                for slot, shape in copies:
                    pltpu.make_async_copy(sizes[shape], sizes[shape], s_all.at[slot]).wait()


def body(embeddings, pair, logit_scale):
    vmem = pl.BlockSpec(memory_space=pltpu.VMEM)
    smem = pl.BlockSpec(memory_space=pltpu.SMEM)
    dma = pltpu.SemaphoreType.DMA
    scratch = [
        ((TOK, D), bf16),
        ((HALF, D), bf16),
        ((8, 2, HALF, D), bf16),
        ((8, TOK, D), bf16),
        ((8, 2, 8, TOK), jnp.int32),
        ((8, TOK, WIDE), f32),
        ((8, TOK, WIDE), bf16),
        ((8, TOK, D), f32),
        ((8, TOK, D), bf16),
        ((2, 2, QUART, D), bf16),
        ((2, 2, 2, QUART, D), bf16),
        ((2, QUART, D), bf16),
        ((2, 2, QUART, D), bf16),
        ((4, 2, 2, QUART, D), bf16),
        ((4, 2, QUART, D), bf16),
        ((2, QUART, D), bf16),
        ((2, 2, QUART, D), bf16),
        ((8, 2, HALF, D), f32),
        ((8, 2, HALF, D), bf16),
        ((8, HALF, D), bf16),
        ((4, HALF, D), bf16),
        ((4, HALF, D), bf16),
        ((3, 8, TOK), f32),
        ((16, 8, TOK), f32),
        ((16, 8, TOK), f32),
        ((2, 8, TOK), f32),
        ((2, 8, TOK), f32),
        ((16, 8, TOK), f32),
        ((16, 8, TOK), f32),
        ((HALF, D), bf16),
        ((HALF, D), bf16),
    ]
    sems = [
        (1,), (SENDS,), (8, 4), (8, 2), (8,), (16,), (2,), (16,), (16,), (16,), (16,),
        (2,), (2, 2), (2,), (2, 2), (4, 2, 2), (4, 2), (2,), (2, 2), (4,), (4, 2), (4, 2), (1,),
    ]
    return pl.pallas_call(
        kernel,
        out_shape=(
            jax.ShapeDtypeStruct((1, TOK, D), bf16),
            jax.ShapeDtypeStruct((1,), f32),
            jax.ShapeDtypeStruct((1,), f32),
        ),
        in_specs=[smem, pl.BlockSpec(memory_space=pl.ANY), vmem],
        out_specs=(vmem, smem, smem),
        scratch_shapes=[pltpu.VMEM(shape, dtype) for shape, dtype in scratch] + [dma(shape) for shape in sems],
        compiler_params=pltpu.CompilerParams(
            collective_id=0, has_side_effects=True, vmem_limit_bytes=56 * 2 ** 20
        ),
        cost_estimate=pl.CostEstimate(flops=6 * WIDE * WIDE * D, bytes_accessed=2 ** 20, transcendentals=2 ** 20),
        name="contrastive",
    )(
        logit_scale.astype(f32).reshape(1),
        embeddings,
        pair.reshape(1, TOK),
    )


def solution(mesh):
    placed = (P("tower", "blk", None), P("blk"), P())
    return jax.shard_map(
        body,
        mesh=mesh,
        in_specs=placed,
        out_specs=(P("tower", "blk", None), P("tower"), P("tower")),
        check_vma=False,
    )
```

time: 82.4 us -> 75.5 us (0.916)
  Pallas kernels: 74.6 us -> 68.9 us
  local copies, waits for them, and re-layouts: 2.89 us -> 1.65 us
    pallas_call x1, Pallas kernels: 74.6 us -> 68.9 us  [body(): pl.pallas_call(kernel, out_shape=(jax.ShapeDtypeStruct((1, TOK, D), bf16)...]
    unnamed x3 -> x1, local copies, waits for them, and re-layouts: 2.29 us -> 1.65 us
where the time goes in v3:
time: 75.5 us; the launch traced here: 75.3 us
  Pallas kernels  68.9 us (91%)
  between operations  4.79 us (6%)
  local copies, waits for them, and re-layouts  1.65 us (2%)
    pallas_call x1, Pallas kernels, body(): pl.pallas_call(kernel, out_shape=(jax.ShapeDtypeStruct((1, TOK, D), bf16)...  68.9 us
    unnamed x1, local copies, waits for them, and re-layouts  1.65 us

profile of v3, /device:TPU:1, one launch (start us, length us, event | category | flops | bytes accessed | tf_op | source)
XLA Modules:
  0.0 75.3 jit_solution(7897014242547386259)
XLA Ops:
  1.3 68.9 %contrastive.1 = (bf16[1,128,896]{2,1,0:T(8,128)(2,1)}, f32[1]{0:T(128)}, f32[1]{0:T(128)}) custom-call(f32[1]{0:T(128)} %bitcast.2.scale_ref, bf16[1,128,896]{2,1,0:T(8,128)(2,1)} %emb_hbm.1, s32[1,128]{1,0:T(1,128)} %bitcast.3), custom_call_target="tpu_custom_call" | custom-call | flops 5637144576 | bytes 1048576 | tf_op jit(solution)/shard_map/contrastive/pallas_call | solution.py:678
  70.1 1.6 %copy.10 = bf16[1,128,896]{2,1,0:T(8,128)(2,1)} copy(bf16[1,128,896]{2,1,0:T(8,128)(2,1)} %get-tuple-element.6) | data formatting | bytes 458752

commit v4 on v3

v4 whole, which is shorter than its diff:
```python
import jax
import jax.numpy as jnp
from jax import lax
from jax.experimental import pallas as pl
from jax.experimental.pallas import tpu as pltpu
from jax.sharding import PartitionSpec as P

eps = 1e-06
TOK = 128
D = 896
TOKENS = 16384
NY, NXH, NZ, NC = 4, 2, 8, 2
HALF, QUART = TOK // 2, TOK // 4
WIDE = 8 * TOK
f32 = jnp.float32
bf16 = jnp.bfloat16
MESH = pl.DeviceIdType.MESH
STEPS = 9
WAVES = 2
DIRECT = 0
DRAINS = 0
ORDER = 1
SCAL = 0
SCAL2 = 1
SENDS = 48


def device(t, y, xh, z, c):
    return (t, ((y * NXH + xh) * NZ + z) * NC + c)


def kernel(
    scale_ref, emb_hbm, pair_ref,
    out_ref, loss_ref, sgrad_ref,
    emb_ref, own, images, texts, pairs, exps, weights,
    text_part, text_send, ra_one, ra_two, ra_x, ra_fin, rb_odd, rb_even, rb_one, rb_two,
    image_part, image_send, image_sib, image_right, image_left, image_first,
    z_row, e_row, columns, pair_rows, hits, stat_send, z_img_all, z_txt_all, e_sums, scal_send, scal_z, scal_p, fin_send, fin_recv,
    s_in, s_all, r_txt, r_img, r_sib, r_pair, r_x, r_zi, r_zt, r_sz, r_sp,
    r_a1, r_a2, r_ax, r_af, r_bo, r_be, r_b1, r_b2, r_is, r_ir, r_il, r_fin, r_far, r_i0,
):
    t = lax.axis_index("tower")
    b = lax.axis_index("blk")
    c = b % 2
    z = (b // 2) % 8
    xh = (b // 16) % 2
    y = b // 32
    odd = t == 1
    even = t == 0
    line_rank = z * 2 + c
    plane_rank = (t * 4 + y) * 2 + xh
    me = y * 2 + xh
    scale = scale_ref[0]
    y_up, y_dn, y_far = (y + 1) % 4, (y + 3) % 4, (y + 2) % 4
    xo = 1 - xh

    conds = {"all": None, "odd": odd, "even": even}
    pending = {name: {} for name in conds}
    count = [0]

    def when(name):
        if name == "all":
            return lambda fn: fn()
        return pl.when(conds[name])

    def send(name, src, dst, rsem, target, batch=""):
        groups = pending[name].setdefault((src.shape, batch), [])
        if not groups or groups[-1][1] == (4 if len(src.shape) == 3 else 15 if src.shape[0] == 8 else 8):
            groups.append([count[0], 0])
            count[0] += 1
        groups[-1][1] += 1
        pltpu.make_async_remote_copy(
            src_ref=src, dst_ref=dst, send_sem=s_all.at[groups[-1][0]], recv_sem=rsem,
            device_id=target, device_id_type=MESH,
        ).start()

    def drain(name, batch=None):
        for key in [k for k in pending[name] if batch is None or k[1] == batch]:
            shape = key[0]
            for slot, copies in pending[name].pop(key):
                if len(shape) == 3:
                    like = texts.at[0:2 * copies, 0:shape[1]]
                elif shape[0] == 8:
                    like = z_img_all.at[0:copies]
                else:
                    like = texts.at[0:copies, 0:shape[0]]
                pltpu.make_async_copy(like, like, s_all.at[slot]).wait()

    def landed(dst, rsem):
        pltpu.make_async_copy(dst, dst, rsem).wait()

    up = device(t, y_up, xh, z, c)
    dn = device(t, y_dn, xh, z, c)
    zp = device(t, y, xh, (z + 1) % 8, c)
    zm = device(t, y, xh, (z + 7) % 8, c)
    sibling = device(t, y, xh, z, 1 - c)
    zp_sibling = device(t, y, xh, (z + 1) % 8, 1 - c)
    zm_sibling = device(t, y, xh, (z + 7) % 8, 1 - c)
    across = [device(1 - t, y, 0, z, c), device(1 - t, y, 1, z, c)]
    partner = device(1 - t, y, xh, z, c)
    partner_zp = device(1 - t, y, xh, (z + 1) % 8, c)
    partner_zm = device(1 - t, y, xh, (z + 7) % 8, c)
    line_peers = [
        device(t, y, xh, (z + dz) % 8, (c + dc) % 2)
        for dz in (4, 3, 5, 2, 6, 1, 7, 0) for dc in (0, 1) if dz or dc
    ]
    plane_peers = [
        device((t + dt) % 2, (y + dy) % 4, (xh + dx) % 2, z, c)
        for dy in (2, 1, 3, 0) for dx in (1, 0) for dt in (0, 1) if dy or dx or dt
    ]

    fetch = pltpu.make_async_copy(emb_hbm.at[0], emb_ref, s_in.at[0])
    fetch.start()
    barrier = pltpu.get_barrier_semaphore()
    for peer in (up, dn, zp, zm, sibling, across[0], across[1], partner_zp, partner_zm):
        pl.semaphore_signal(barrier, inc=1, device_id=peer, device_id_type=MESH)
    fetch.wait()

    def normal(part):
        wide = emb_ref[part].astype(f32)
        lengths = jnp.sqrt(jnp.sum(wide * wide, axis=1, keepdims=True) + eps)
        return wide / lengths, lengths

    lower, upper = slice(0, HALF), slice(HALF, TOK)
    unit_low = normal(lower)[0].astype(bf16)
    unit_high = normal(upper)[0].astype(bf16)

    @when("odd")
    def _():
        texts[me, lower] = unit_low
        texts[me, upper] = unit_high

    @when("even")
    def _():
        images[z, c] = unit_low
        own[...] = unit_high

    pairs[line_rank] = jnp.broadcast_to(pair_ref[...], (8, TOK))
    pl.semaphore_wait(barrier, 9)

    def rows(index, quarter):
        return texts.at[index, pl.ds(quarter * QUART, QUART)]

    def tsend(name, index, quarter, target, batch=""):
        send(name, rows(index, quarter), rows(index, quarter), r_txt.at[index, quarter], target, batch)

    def twait(index, quarter):
        landed(rows(index, quarter), r_txt.at[index, quarter])

    size = HALF // WAVES

    def piece(slot, w):
        return images.at[slot, c, pl.ds(w * size, size)]

    def isend(name, slot, w, target):
        send(name, piece(slot, w), piece(slot, w), r_img.at[slot, w], target)

    def iwait(slot, w):
        landed(piece(slot, w), r_img.at[slot, w])

    def to_sibling(name, slot):
        send(name, images.at[slot, c], images.at[slot, c], r_sib.at[slot], sibling)

    def image_hop(name, k):
        left, right = (z + 8 - k) % 8, (z + k) % 8
        for w in range(WAVES):
            iwait(left, w)
            if k < 3 or w < WAVES // 2:
                isend(name, left, w, zp)
            if k == 3 and w < WAVES // 2:
                send(name, piece(left, w), piece(left, w), r_far.at[w], zp_sibling)
            iwait(right, w)
            if k < 3 or w >= WAVES // 2:
                isend(name, right, w, zm)
            if k == 3 and w >= WAVES // 2:
                send(name, piece(right, w), piece(right, w), r_far.at[w], zm_sibling)
        to_sibling(name, left)
        to_sibling(name, right)

    def image_last(name):
        far = (z + 4) % 8
        for w in range(WAVES):
            iwait(far, w)
            landed(images.at[far, 1 - c, pl.ds(w * size, size)], r_far.at[w])

    def siblings(p):
        for h in range(2):
            landed(images.at[2 * p + h, 1 - c], r_sib.at[2 * p + h])

    half_z = z // 2
    p_far, p_up, p_dn, p_own = [(half_z + k) % 4 for k in (2, 1, 3, 0)]

    if STEPS > 1:
        @when("even")
        def _():
            n = "even"
            first, second = device(t, (y + 1 + 2 * xh) % 4, xh, z, c), device(t, (y + 1 + 2 * xo) % 4, xh, z, c)

            def mine(w):
                return own.at[pl.ds(w * size, size)]

            for w in range(WAVES):
                isend(n, z, w, zp)
                isend(n, z, w, zm)
                if DIRECT:
                    send(n, mine(w), piece(z, w), r_img.at[z, w], partner_zp)
                    send(n, mine(w), piece(z, w), r_img.at[z, w], partner_zm)
                else:
                    send(n, mine(w), piece(z, w), r_x.at[w], partner)
            to_sibling(n, z)
            image_hop(n, 1)
            for q in range(2):
                index = y * 2 + q
                twait(index, xh)
                tsend(n, index, xh, across[1 - q])
                tsend(n, index, xh, first)
            for q in range(2):
                index = y * 2 + q
                twait(index, xo)
                tsend(n, index, xo, second)
            for q in range(2):
                index = y * 2 + q
                twait(index, 2 + xh)
                tsend(n, index, 2 + xh, across[1 - q])
            for q in range(2):
                index = y * 2 + q
                tsend(n, index, xh, second)
                tsend(n, index, xo, first)
            ya, yb = (y + 3 + 2 * xh) % 4, (y + 1 + 2 * xh) % 4
            for q in range(2):
                index = ya * 2 + q
                twait(index, 2 + xh)
                tsend(n, index, 2 + xh, across[1 - q])
            image_hop(n, 2)
            for q in range(2):
                index = yb * 2 + q
                twait(index, 2 + xh)
                tsend(n, index, 2 + xh, across[1 - q])
            for w in range(WAVES if DIRECT else 0):
                send(n, mine(w), piece(z, w), r_x.at[w], partner)
            for q in range(2):
                twait(y_dn * 2 + q, 0)
                tsend(n, y_dn * 2 + q, 0, up)
                twait(y_up * 2 + q, 1)
                tsend(n, y_up * 2 + q, 1, dn)
            for q in range(2):
                index = y_far * 2 + q
                twait(index, 2 + xh)
                tsend(n, index, 2 + xh, across[1 - q])
            image_hop(n, 3)
            for q in range(2):
                twait(y_dn * 2 + q, 1)
                twait(y_up * 2 + q, 0)
                for k in range(2):
                    twait(y_far * 2 + q, k)
                for ya in (y, y_dn, y_up, y_far):
                    twait(ya * 2 + q, 2 + xo)

        @when("odd")
        def _():
            n = "odd"
            mine, below, above, far = me, y_dn * 2 + xh, y_up * 2 + xh, y_far * 2 + xh
            other = y * 2 + xo

            def relayed(index, k):
                tsend(n, index, 2 + k, across[k])

            def kept(index):
                for e in range(2):
                    tsend(n, index, 3 - e, across[e])

            for e in range(2):
                tsend(n, mine, e, across[e], "s")
            tsend(n, mine, 2, up, "s")
            tsend(n, mine, 3, dn, "s")
            if DRAINS > 0:
                drain(n, "s")
            for e in range(2):
                tsend(n, mine, 1 - e, across[e], "s")
            tsend(n, mine, 3, up, "s")
            tsend(n, mine, 2, dn, "s")
            if DRAINS > 1:
                drain(n, "s")
            if not DIRECT:
                for w in range(WAVES):
                    landed(piece(z, w), r_x.at[w])
                    isend(n, z, w, zp)
                    isend(n, z, w, zm)
                to_sibling(n, z)
            for e in range(2):
                relayed(mine, e)
            tsend(n, mine, 0, up)
            tsend(n, mine, 1, dn)
            twait(below, 2)
            tsend(n, below, 2, up)
            relayed(below, 0)
            twait(above, 3)
            tsend(n, above, 3, dn)
            relayed(above, 1)
            tsend(n, mine, 1, up)
            tsend(n, mine, 0, dn)
            twait(below, 3)
            relayed(below, 1)
            twait(above, 2)
            relayed(above, 0)
            image_hop(n, 1)
            twait(below, 0)
            tsend(n, below, 0, up)
            twait(above, 1)
            tsend(n, above, 1, dn)
            twait(far, 2)
            relayed(far, 0)
            twait(far, 3)
            relayed(far, 1)
            twait(other, 0)
            tsend(n, other, 0, up)
            twait(other, 1)
            tsend(n, other, 1, dn)
            kept(mine)
            tsend(n, other, 1, up)
            tsend(n, other, 0, dn)
            kept(below)
            kept(above)
            image_hop(n, 2)
            kept(far)
            twait(y_dn * 2 + xo, 0)
            tsend(n, y_dn * 2 + xo, 0, up)
            twait(y_up * 2 + xo, 1)
            tsend(n, y_up * 2 + xo, 1, dn)
            for q in (xh, xo):
                twait(y_dn * 2 + q, 1)
                twait(y_up * 2 + q, 0)
                for k in range(2):
                    twait(y_far * 2 + q, k)
            for ya in (y, y_dn, y_up, y_far):
                for k in range(2):
                    twait(ya * 2 + xo, 2 + k)
            if DIRECT:
                for w in range(WAVES):
                    landed(piece(z, w), r_x.at[w])
                to_sibling(n, z)

        siblings(p_own)

    def first_id(index):
        return ((index * 8 + z) * 2 + c) * TOK

    sub_ids = lax.broadcasted_iota(jnp.int32, (TOK, 1), 0)

    def total(x):
        return jnp.sum(jnp.sum(x, axis=0, keepdims=True), axis=1, keepdims=True)

    if STEPS > 2:
        all_texts = texts[...].reshape(WIDE, D)

        def stats(p, first):
            two = images[pl.ds(2 * p, 2)].reshape(2 * TOK, D)
            dots = lax.dot_general(all_texts, two, (((1,), (1,)), ((), ())), preferred_element_type=f32)
            scores = scale * dots
            ex = jnp.exp(scores - scale)
            exps[:, :, pl.ds(pl.multiple_of(p * 2 * TOK, 2 * TOK), 2 * TOK)] = ex.reshape(8, TOK, 2 * TOK)
            es = ex * scores
            z_sum = jnp.sum(ex, axis=0, keepdims=True)
            e_sum = jnp.sum(es, axis=0, keepdims=True)
            for h in range(2):
                part = slice(h * TOK, (h + 1) * TOK)
                stat_send[0, pl.ds(2 * p + h, 1), :] = z_sum[:, part]
                e_sums[pl.ds(2 * p + h, 1), :] = e_sum[:, part]
            zr = (ex[:, 0:TOK] + ex[:, TOK:]).reshape(8, TOK, TOK)
            er = (es[:, 0:TOK] + es[:, TOK:]).reshape(8, TOK, TOK)
            z_row[...] = zr if first else z_row[...] + zr
            e_row[...] = er if first else e_row[...] + er

        stats(p_own, True)

        @when("odd")
        def _():
            image_hop("odd", 3)

        for p in (p_up, p_dn):
            siblings(p)
            stats(p, False)

        @when("even")
        def _():
            image_last("even")

        @when("odd")
        def _():
            image_last("odd")

        for peer in line_peers if STEPS > 3 else ():
            send("all", pairs.at[line_rank], pairs.at[line_rank], r_pair.at[0], peer)
        near_far = (z + 3 + 2 * ((z + 1) % 2)) % 8
        landed(images.at[near_far, 1 - c], r_sib.at[near_far])
        stats(p_far, False)
        for k in range(8):
            stat_send[1, k:k + 1, :] = jnp.sum(z_row[k].T, axis=0, keepdims=True)
        all_images = images[...].reshape(WIDE, D)

    if STEPS > 3:
        for peer in line_peers:
            send("all", stat_send.at[0], z_img_all.at[line_rank], r_zi.at[0], peer)
        for peer in plane_peers:
            send("all", stat_send.at[1], z_txt_all.at[plane_rank], r_zt.at[0], peer)
        z_img_all[line_rank] = stat_send[0]
        z_txt_all[plane_rank] = stat_send[1]
        landed(pairs.at[0:15], r_pair.at[0])

        def own_half(k, core):
            line = pairs[2 * k + core, 0:1]
            return jnp.where(odd, line[:, HALF:TOK], line[:, 0:HALF])

        for k in range(8):
            pair_rows[k:k + 1, :] = jnp.concatenate([own_half(k, core) for core in range(2)], axis=1)
        landed(z_img_all.at[0:15], r_zi.at[0])
        landed(z_txt_all.at[0:15], r_zt.at[0])
        z_img = jnp.sum(z_img_all[...], axis=0)
        z_txt = jnp.sum(z_txt_all[...], axis=0)

    if STEPS > 4:
        stat_send[3] = 0.5 / z_img
        stat_send[2] = 0.5 / z_txt
        for k in range(8):
            columns[k] = jnp.broadcast_to(stat_send[2, k:k + 1, :], (TOK, TOK)).T

        def weigh(p):
            lanes = pl.ds(pl.multiple_of(p * 2 * TOK, 2 * TOK), 2 * TOK)
            img = jnp.concatenate([stat_send[3, pl.ds(2 * p + h, 1), :] for h in range(2)], axis=1)
            partners = jnp.concatenate([pair_rows[pl.ds(2 * p + h, 1), :] for h in range(2)], axis=1)

            def step(index, carry):
                column = columns[index]
                ids = first_id(index) + sub_ids
                match = partners == ids
                ex = exps[index, :, lanes]
                value = ex * (img + jnp.concatenate([column, column], axis=1))
                weights[index, :, lanes] = (value - jnp.where(match, 1.0, 0.0)).astype(bf16)
                return carry + jnp.sum(jnp.where(match, ex, 0.0), axis=0, keepdims=True)

            hit = lax.fori_loop(0, 8, step, jnp.zeros((1, 2 * TOK), f32))
            for h in range(2):
                hits[pl.ds(2 * p + h, 1), :] = hit[:, h * TOK:(h + 1) * TOK]

        weigh(p_far)

    def text_block(ya):
        pair_of = pl.ds(2 * ya, 2)
        two = weights[pair_of].reshape(2 * TOK, WIDE)
        part = jnp.dot(two, all_images, preferred_element_type=f32)
        text_part[pair_of] = part.reshape(2, TOK, D)

    def quart(k):
        return pl.ds(k * QUART, QUART)

    def stage(index, k):
        text_send[index, quart(k)] = text_part[index, quart(k)].astype(bf16)
        return text_send.at[index, quart(k)]

    def stage_two(ya, k):
        for q in range(2):
            stage(ya * 2 + q, k)
        return text_send.at[pl.ds(2 * ya, 2), quart(k)]

    def add(index, k, value):
        text_part[index, quart(k)] = text_part[index, quart(k)] + value.astype(f32)

    def give_b(slot, ya):
        for k in range(2):
            send("odd", stage(ya * 2 + xo, 2 + k), rb_even.at[slot, xh], r_be.at[slot, xh], across[k])

    def free_b(slot, ya):
        for q in range(2):
            send("even", stage(ya * 2 + q, 2 + xo), rb_odd.at[slot, xh, 0], r_bo.at[slot, xh, 0], across[q])

    def pass_b(slot, ya):
        for q in range(2):
            index = ya * 2 + q
            landed(rb_even.at[slot, 1 - q], r_be.at[slot, 1 - q])
            add(index, 2 + xh, rb_even[slot, 1 - q])
            send("even", stage(index, 2 + xh), rb_odd.at[slot, xh, 1], r_bo.at[slot, xh, 1], across[q])

    def take_b(slot, ya):
        index = ya * 2 + xh
        for part in range(2):
            for e in range(2):
                landed(rb_odd.at[slot, e, part], r_bo.at[slot, e, part])
                add(index, 2 + (e if part else 1 - e), rb_odd[slot, e, part])

    def image_block(p, with_sibling=True):
        lanes = pl.ds(pl.multiple_of(p * 2 * TOK, 2 * TOK), 2 * TOK)
        part = lax.dot_general(
            weights[:, :, lanes].reshape(WIDE, 2 * TOK), texts[...].reshape(WIDE, D),
            (((0,), (0,)), ((), ())), preferred_element_type=f32,
        )
        both = pl.ds(2 * p, 2)
        image_part[both] = part.reshape(2, 2, HALF, D)
        if with_sibling:
            image_send[both, 1 - c] = image_part[both, 1 - c].astype(bf16)
            send("all", image_send.at[both, 1 - c], image_sib.at[both], r_is.at[p], sibling)

    def swap_near_far():
        image_send[near_far, 1 - c] = image_part[near_far, 1 - c].astype(bf16)
        send("all", image_send.at[near_far, 1 - c], image_sib.at[near_far], r_is.at[p_far], sibling)

    def add_near_far():
        landed(image_sib.at[near_far], r_is.at[p_far])
        image_part[near_far, c] = image_part[near_far, c] + image_sib[near_far].astype(f32)

    def add_sibling(p):
        both = pl.ds(2 * p, 2)
        landed(image_sib.at[both], r_is.at[p])
        image_part[both, c] = image_part[both, c] + image_sib[both].astype(f32)

    def source_of(slot, h):
        return image_send.at[slot, c, quart(h)]

    def ring_send(m, h, right):
        hops = 4 - m
        slot = (z + hops) % 8 if right else (z + 8 - hops) % 8
        into = image_right if right else image_left
        sem = r_ir if right else r_il
        value = image_part[slot, c, quart(h)]
        if m == 1 and h == (0 if right else 1):
            for core in range(2):
                landed(image_first.at[h, core], r_i0.at[h, core])
                value = value + image_first[h, core].astype(f32)
        if m > 1:
            landed(into.at[m - 1, quart(h)], sem.at[m - 1, h])
            value = value + into[m - 1, quart(h)].astype(f32)
        image_send[slot, c, quart(h)] = value.astype(bf16)
        if m < 3:
            send("all", source_of(slot, h), into.at[m, quart(h)], sem.at[m, h], zp if right else zm)
            return
        way = 0 if right else 1

        @when("even")
        def _():
            send("even", source_of(slot, h), into.at[m, quart(h)], sem.at[m, h], zp if right else zm)

        @when("odd")
        def _():
            send(
                "odd", source_of(slot, h), fin_recv.at[way, quart(h)], r_fin.at[way, h],
                partner_zp if right else partner_zm,
            )

    if STEPS > 5:
        def spread(slot, ya):
            @when("odd")
            def _():
                give_b(slot, ya)

            @when("even")
            def _():
                free_b(slot, ya)

        def pass_on(slot, ya):
            @when("even")
            def _():
                pass_b(slot, ya)

        def hop_a(way, ya, target):
            landed(ra_one.at[way], r_a1.at[way])
            for q in range(2):
                add(ya * 2 + q, way, ra_one[way, q])
            send("all", stage_two(ya, way), ra_two.at[way, 1], r_a2.at[way, 1], target)

        def r1():
            send("all", stage_two(y_far, 0), ra_one.at[0], r_a1.at[0], up)
            send("all", stage_two(y_far, 1), ra_one.at[1], r_a1.at[1], dn)

        def m0():
            far = (z + 4) % 8
            for way, right, left in ((0, zp, zp_sibling), (1, zm, zm_sibling)):
                for core, target in ((c, right), (1 - c, left)):
                    image_send[far, core, quart(way)] = image_part[far, core, quart(way)].astype(bf16)
                    send(
                        "all", image_send.at[far, core, quart(way)], image_first.at[way, c], r_i0.at[way, c], target
                    )

        def m1_free():
            add_near_far()
            add_sibling(p_up)
            add_sibling(p_dn)
            ring_send(1, 1, True)
            ring_send(1, 0, False)

        def m1():
            ring_send(1, 0, True)
            ring_send(1, 1, False)

        def far_b():
            @when("odd")
            def _():
                take_b(0, y_far)
                send("odd", stage(y_far * 2 + xh, 2), rb_one.at[0], r_b1.at[0], up)
                send("odd", stage(y_far * 2 + xh, 3), rb_one.at[1], r_b1.at[1], dn)

        def free_a(way, ya, target):
            send("all", stage_two(ya, 1 - way), ra_two.at[way, 0], r_a2.at[way, 0], target)

        def m2():
            for h in (1, 0):
                ring_send(2, h, True)
                ring_send(2, 1 - h, False)

        T = lambda ya, slot: (text_block(ya), spread(slot, ya))
        I = image_block
        def rest():
            for p in (p_up, p_dn, p_own):
                weigh(p)

        if ORDER == 1:
            I(p_far, False); m0(); swap_near_far(); rest(); T(y_far, 0); r1(); I(p_up); I(p_dn); T(y_dn, 1); m1_free(); free_a(1, y_dn, dn)
            T(y_up, 2); free_a(0, y_up, up); m1(); pass_on(0, y_far); hop_a(0, y_up, up); hop_a(1, y_dn, dn); T(y, 3)
            pass_on(1, y_dn); pass_on(2, y_up); I(p_own); far_b(); pass_on(3, y); m2()
        if ORDER == 2:
            I(p_far, False); m0(); swap_near_far(); rest(); T(y_far, 0); r1(); I(p_up); T(y_dn, 1); I(p_dn); m1_free(); free_a(1, y_dn, dn)
            T(y_up, 2); free_a(0, y_up, up); pass_on(0, y_far); m1(); T(y, 3); hop_a(0, y_up, up); hop_a(1, y_dn, dn)
            pass_on(1, y_dn); I(p_own); pass_on(2, y_up); pass_on(3, y); m2(); far_b()
        if ORDER == 3:
            I(p_far, False); m0(); swap_near_far(); rest(); T(y_far, 0); r1(); I(p_up); I(p_dn); m1_free(); T(y_dn, 1); free_a(1, y_dn, dn)
            T(y_up, 2); free_a(0, y_up, up); T(y, 3); m1(); pass_on(0, y_far); hop_a(0, y_up, up); hop_a(1, y_dn, dn)
            pass_on(1, y_dn); pass_on(2, y_up); I(p_own); far_b(); pass_on(3, y); m2()

        lane = lax.broadcasted_iota(jnp.int32, (8, TOK), 1)

        def scalars():
            log_img = total(jnp.log(z_img))
            log_txt = total(jnp.log(z_txt))
            t_img = total(e_sums[...] / z_img)
            t_acc = e_row[0] * columns[0]
            for k in range(1, 8):
                t_acc = t_acc + e_row[k] * columns[k]
            t_txt = 2.0 * total(t_acc)
            hit = hits[...]
            found = hit > 0.0
            matched = total(jnp.where(found, jnp.log(jnp.where(found, hit, 1.0)) + scale, 0.0))
            scal_send[0] = jnp.where(
                lane == 0, log_txt,
                jnp.where(lane == 1, t_img, jnp.where(lane == 2, t_txt, jnp.where(lane == 3, matched, 0.0))),
            )
            for peer in line_peers:
                send("all", scal_send.at[0], scal_z.at[line_rank], r_sz.at[0], peer)
            scal_z[line_rank] = scal_send[0]
            return log_img

        if SCAL == 0:
            log_img = scalars()
        add_sibling(p_own)

        @when("odd")
        def _():
            fin_send[...] = image_part[z, c].astype(bf16)
            send("odd", fin_send, fin_recv.at[2], r_fin.at[2, 0], partner)

        if SCAL == 1:
            log_img = scalars()

        for part in range(2):
            for way in range(2):
                landed(ra_two.at[way, part], r_a2.at[way, part])
                for q in range(2):
                    add(y * 2 + q, way if part else 1 - way, ra_two[way, part, q])

        @when("odd")
        def _():
            for k in range(2):
                send("odd", stage(y * 2 + xo, k), ra_x.at[xh], r_ax.at[xh], across[k])
            take_b(1, y_dn)
            take_b(2, y_up)
            send("odd", stage(y_up * 2 + xh, 3), rb_two.at[0, 0], r_b2.at[0, 0], up)
            send("odd", stage(y_dn * 2 + xh, 2), rb_two.at[1, 0], r_b2.at[1, 0], dn)
            for way, ya, target in ((0, y_up, up), (1, y_dn, dn)):
                landed(rb_one.at[way], r_b1.at[way])
                add(ya * 2 + xh, 2 + way, rb_one[way])
                send("odd", stage(ya * 2 + xh, 2 + way), rb_two.at[way, 1], r_b2.at[way, 1], target)

        @when("even")
        def _():
            for q in range(2):
                send("even", stage(y * 2 + q, xo), ra_fin.at[xh, 0], r_af.at[xh, 0], across[q])

        def second_step():
            landed(scal_z.at[0:15], r_sz.at[0])
            line_sum = jnp.sum(scal_z[...], axis=0)
            scal_send[1] = jnp.where(lane == 4, log_img, line_sum)
            for peer in plane_peers:
                send("all", scal_send.at[1], scal_p.at[plane_rank], r_sp.at[0], peer)
            scal_p[plane_rank] = scal_send[1]
            return line_sum

        if SCAL2 == 1:
            line_sum = second_step()

        for h in (1, 0):
            ring_send(3, h, True)
            ring_send(3, 1 - h, False)

        @when("even")
        def _():
            for q in range(2):
                landed(ra_x.at[1 - q], r_ax.at[1 - q])
                add(y * 2 + q, xh, ra_x[1 - q])
                send("even", stage(y * 2 + q, xh), ra_fin.at[xh, 1], r_af.at[xh, 1], across[q])

        if SCAL2 == 0:
            line_sum = second_step()

        def finish(part, grads):
            unit32, lengths = normal(part)
            grads = scale * grads
            inner = jnp.sum(unit32 * grads, axis=1, keepdims=True)
            out_ref[0, part] = ((grads - unit32 * inner) / lengths).astype(bf16)

        @when("odd")
        def _():
            take_b(3, y)

        @when("odd")
        def _():
            for part in range(2):
                for way in range(2):
                    landed(rb_two.at[way, part], r_b2.at[way, part])
                    add(me, 2 + (way if part else 1 - way), rb_two[way, part])
            finish(upper, text_part[me, upper])
            for part in range(2):
                for e in range(2):
                    landed(ra_fin.at[e, part], r_af.at[e, part])
                    add(me, e if part else 1 - e, ra_fin[e, part])
            finish(lower, text_part[me, lower])

        @when("even")
        def _():
            for h in range(2):
                landed(image_right.at[3, quart(h)], r_ir.at[3, h])
                landed(image_left.at[3, quart(h)], r_il.at[3, h])
            finish(lower, image_part[z, c] + image_right[3].astype(f32) + image_left[3].astype(f32))
            landed(fin_recv.at[2], r_fin.at[2, 0])
            for h in range(2):
                landed(fin_recv.at[0, quart(h)], r_fin.at[0, h])
                landed(fin_recv.at[1, quart(h)], r_fin.at[1, h])
            finish(
                upper,
                fin_recv[0].astype(f32) + fin_recv[1].astype(f32) + fin_recv[2].astype(f32),
            )

        landed(scal_p.at[0:15], r_sp.at[0])
        all_sum = jnp.sum(scal_p[...], axis=0)

        def pick(x, k):
            return jnp.sum(jnp.where(lane[0:1] == k, x[0:1], 0.0))

        log_all = jnp.where(odd, pick(line_sum, 0), pick(all_sum, 4))
        t_all = jnp.where(odd, pick(all_sum, 2), pick(all_sum, 1))
        p_all = pick(all_sum, 3)
        loss_ref[0] = (scale * TOKENS + log_all - p_all) * (1.0 / (2 * TOKENS))
        sgrad_ref[0] = (t_all - p_all) / scale * (1.0 / (2 * TOKENS))

    for name in pending:
        if pending[name]:
            @when(name)
            def _():
                drain(name)


def body(embeddings, pair, logit_scale):
    vmem = pl.BlockSpec(memory_space=pltpu.VMEM)
    smem = pl.BlockSpec(memory_space=pltpu.SMEM)
    dma = pltpu.SemaphoreType.DMA
    scratch = [
        ((TOK, D), bf16),
        ((HALF, D), bf16),
        ((8, 2, HALF, D), bf16),
        ((8, TOK, D), bf16),
        ((16, 8, TOK), jnp.int32),
        ((8, TOK, WIDE), f32),
        ((8, TOK, WIDE), bf16),
        ((8, TOK, D), f32),
        ((8, TOK, D), bf16),
        ((2, 2, QUART, D), bf16),
        ((2, 2, 2, QUART, D), bf16),
        ((2, QUART, D), bf16),
        ((2, 2, QUART, D), bf16),
        ((4, 2, 2, QUART, D), bf16),
        ((4, 2, QUART, D), bf16),
        ((2, QUART, D), bf16),
        ((2, 2, QUART, D), bf16),
        ((8, 2, HALF, D), f32),
        ((8, 2, HALF, D), bf16),
        ((8, HALF, D), bf16),
        ((4, HALF, D), bf16),
        ((4, HALF, D), bf16),
        ((2, 2, QUART, D), bf16),
        ((8, TOK, TOK), f32),
        ((8, TOK, TOK), f32),
        ((8, TOK, TOK), f32),
        ((8, TOK), jnp.int32),
        ((8, TOK), f32),
        ((4, 8, TOK), f32),
        ((16, 8, TOK), f32),
        ((16, 8, TOK), f32),
        ((8, TOK), f32),
        ((2, 8, TOK), f32),
        ((16, 8, TOK), f32),
        ((16, 8, TOK), f32),
        ((HALF, D), bf16),
        ((3, HALF, D), bf16),
    ]
    sems = [
        (1,), (SENDS,), (8, 4), (8, 4), (8,), (1,), (4,), (1,), (1,), (1,), (1,),
        (2,), (2, 2), (2,), (2, 2), (4, 2, 2), (4, 2), (2,), (2, 2), (4,), (4, 2), (4, 2), (3, 2), (4,), (2, 2),
    ]
    return pl.pallas_call(
        kernel,
        out_shape=(
            jax.ShapeDtypeStruct((1, TOK, D), bf16),
            jax.ShapeDtypeStruct((1,), f32),
            jax.ShapeDtypeStruct((1,), f32),
        ),
        in_specs=[smem, pl.BlockSpec(memory_space=pl.ANY), vmem],
        out_specs=(vmem, smem, smem),
        scratch_shapes=[pltpu.VMEM(shape, dtype) for shape, dtype in scratch] + [dma(shape) for shape in sems],
        compiler_params=pltpu.CompilerParams(
            collective_id=0, has_side_effects=True, vmem_limit_bytes=56 * 2 ** 20
        ),
        cost_estimate=pl.CostEstimate(flops=6 * WIDE * WIDE * D, bytes_accessed=2 ** 20, transcendentals=2 ** 20),
        name="contrastive",
    )(
        logit_scale.astype(f32).reshape(1),
        embeddings,
        pair.reshape(1, TOK),
    )


def solution(mesh):
    placed = (P("tower", "blk", None), P("blk"), P())
    return jax.shard_map(
        body,
        mesh=mesh,
        in_specs=placed,
        out_specs=(P("tower", "blk", None), P("tower"), P("tower")),
        check_vma=False,
    )
```

time: 75.5 us -> 73.8 us (0.977)
  the two profiles are of different devices: /device:TPU:1 before, /device:TPU:2 now
where the time goes in v4:
time: 73.8 us; the launch traced here: 73.7 us
  Pallas kernels  67.2 us (91%)
  between operations  4.79 us (6%)
  local copies, waits for them, and re-layouts  1.65 us (2%)
    pallas_call x1, Pallas kernels, body(): pl.pallas_call(kernel, out_shape=(jax.ShapeDtypeStruct((1, TOK, D), bf16)...  67.2 us
    unnamed x1, local copies, waits for them, and re-layouts  1.65 us

profile of v4, /device:TPU:2, one launch (start us, length us, event | category | flops | bytes accessed | tf_op | source)
XLA Modules:
  0.0 73.7 jit_solution(9284331060912857343)
XLA Ops:
  1.3 67.2 %contrastive.1 = (bf16[1,128,896]{2,1,0:T(8,128)(2,1)}, f32[1]{0:T(128)}, f32[1]{0:T(128)}) custom-call(f32[1]{0:T(128)} %bitcast.2.scale_ref, bf16[1,128,896]{2,1,0:T(8,128)(2,1)} %emb_hbm.1, s32[1,128]{1,0:T(1,128)} %bitcast.3), custom_call_target="tpu_custom_call" | custom-call | flops 5637144576 | bytes 1048576 | tf_op jit(solution)/shard_map/contrastive/pallas_call | solution.py:815
  68.5 1.6 %copy.10 = bf16[1,128,896]{2,1,0:T(8,128)(2,1)} copy(bf16[1,128,896]{2,1,0:T(8,128)(2,1)} %get-tuple-element.6) | data formatting | bytes 458752

commit v5 on v4

--- a/solution.py
+++ b/solution.py
@@ -19,7 +19,8 @@
 WAVES = 2
 DIRECT = 0
 DRAINS = 0
-ORDER = 1
+ORDER = 4
+OUTF = 1
 SCAL = 0
 SCAL2 = 1
 SENDS = 48
@@ -32,11 +33,11 @@
 def kernel(
     scale_ref, emb_hbm, pair_ref,
     out_ref, loss_ref, sgrad_ref,
-    emb_ref, own, images, texts, pairs, exps, weights,
+    emb_ref, own, images, texts, z_msg, exps, weights,
     text_part, text_send, ra_one, ra_two, ra_x, ra_fin, rb_odd, rb_even, rb_one, rb_two,
     image_part, image_send, image_sib, image_right, image_left, image_first,
     z_row, e_row, columns, pair_rows, hits, stat_send, z_img_all, z_txt_all, e_sums, scal_send, scal_z, scal_p, fin_send, fin_recv,
-    s_in, s_all, r_txt, r_img, r_sib, r_pair, r_x, r_zi, r_zt, r_sz, r_sp,
+    s_in, s_all, r_txt, r_img, r_sib, r_x, r_zi, r_zt, r_sz, r_sp,
     r_a1, r_a2, r_ax, r_af, r_bo, r_be, r_b1, r_b2, r_is, r_ir, r_il, r_fin, r_far, r_i0,
 ):
     t = lax.axis_index("tower")
@@ -65,7 +66,7 @@
 
     def send(name, src, dst, rsem, target, batch=""):
         groups = pending[name].setdefault((src.shape, batch), [])
-        if not groups or groups[-1][1] == (4 if len(src.shape) == 3 else 15 if src.shape[0] == 8 else 8):
+        if not groups or groups[-1][1] == (4 if len(src.shape) == 3 else 15 if src.shape[1] == TOK else 8):
             groups.append([count[0], 0])
             count[0] += 1
         groups[-1][1] += 1
@@ -80,8 +81,10 @@
             for slot, copies in pending[name].pop(key):
                 if len(shape) == 3:
                     like = texts.at[0:2 * copies, 0:shape[1]]
-                elif shape[0] == 8:
+                elif shape == (16, TOK):
                     like = z_img_all.at[0:copies]
+                elif shape == (8, TOK):
+                    like = z_txt_all.at[0:copies]
                 else:
                     like = texts.at[0:copies, 0:shape[0]]
                 pltpu.make_async_copy(like, like, s_all.at[slot]).wait()
@@ -135,7 +138,7 @@
         images[z, c] = unit_low
         own[...] = unit_high
 
-    pairs[line_rank] = jnp.broadcast_to(pair_ref[...], (8, TOK))
+    z_msg[8:16, :] = jnp.broadcast_to(pair_ref[...], (8, TOK)).astype(f32)
     pl.semaphore_wait(barrier, 9)
 
     def rows(index, quarter):
@@ -364,7 +367,7 @@
             e_sum = jnp.sum(es, axis=0, keepdims=True)
             for h in range(2):
                 part = slice(h * TOK, (h + 1) * TOK)
-                stat_send[0, pl.ds(2 * p + h, 1), :] = z_sum[:, part]
+                z_msg[pl.ds(2 * p + h, 1), :] = z_sum[:, part]
                 e_sums[pl.ds(2 * p + h, 1), :] = e_sum[:, part]
             zr = (ex[:, 0:TOK] + ex[:, TOK:]).reshape(8, TOK, TOK)
             er = (es[:, 0:TOK] + es[:, TOK:]).reshape(8, TOK, TOK)
@@ -389,33 +392,30 @@
         def _():
             image_last("odd")
 
-        for peer in line_peers if STEPS > 3 else ():
-            send("all", pairs.at[line_rank], pairs.at[line_rank], r_pair.at[0], peer)
         near_far = (z + 3 + 2 * ((z + 1) % 2)) % 8
         landed(images.at[near_far, 1 - c], r_sib.at[near_far])
         stats(p_far, False)
+        for peer in line_peers if STEPS > 3 else ():
+            send("all", z_msg, z_img_all.at[line_rank], r_zi.at[0], peer)
         for k in range(8):
             stat_send[1, k:k + 1, :] = jnp.sum(z_row[k].T, axis=0, keepdims=True)
         all_images = images[...].reshape(WIDE, D)
 
     if STEPS > 3:
-        for peer in line_peers:
-            send("all", stat_send.at[0], z_img_all.at[line_rank], r_zi.at[0], peer)
         for peer in plane_peers:
             send("all", stat_send.at[1], z_txt_all.at[plane_rank], r_zt.at[0], peer)
-        z_img_all[line_rank] = stat_send[0]
+        z_img_all[line_rank] = z_msg[...]
         z_txt_all[plane_rank] = stat_send[1]
-        landed(pairs.at[0:15], r_pair.at[0])
+        landed(z_img_all.at[0:15], r_zi.at[0])
 
         def own_half(k, core):
-            line = pairs[2 * k + core, 0:1]
-            return jnp.where(odd, line[:, HALF:TOK], line[:, 0:HALF])
+            line = z_img_all[2 * k + core, 8:9]
+            return jnp.where(odd, line[:, HALF:TOK], line[:, 0:HALF]).astype(jnp.int32)
 
         for k in range(8):
             pair_rows[k:k + 1, :] = jnp.concatenate([own_half(k, core) for core in range(2)], axis=1)
-        landed(z_img_all.at[0:15], r_zi.at[0])
         landed(z_txt_all.at[0:15], r_zt.at[0])
-        z_img = jnp.sum(z_img_all[...], axis=0)
+        z_img = jnp.sum(z_img_all[:, 0:8], axis=0)
         z_txt = jnp.sum(z_txt_all[...], axis=0)
 
     if STEPS > 4:
@@ -610,19 +610,6 @@
         def rest():
             for p in (p_up, p_dn, p_own):
                 weigh(p)
-
-        if ORDER == 1:
-            I(p_far, False); m0(); swap_near_far(); rest(); T(y_far, 0); r1(); I(p_up); I(p_dn); T(y_dn, 1); m1_free(); free_a(1, y_dn, dn)
-            T(y_up, 2); free_a(0, y_up, up); m1(); pass_on(0, y_far); hop_a(0, y_up, up); hop_a(1, y_dn, dn); T(y, 3)
-            pass_on(1, y_dn); pass_on(2, y_up); I(p_own); far_b(); pass_on(3, y); m2()
-        if ORDER == 2:
-            I(p_far, False); m0(); swap_near_far(); rest(); T(y_far, 0); r1(); I(p_up); T(y_dn, 1); I(p_dn); m1_free(); free_a(1, y_dn, dn)
-            T(y_up, 2); free_a(0, y_up, up); pass_on(0, y_far); m1(); T(y, 3); hop_a(0, y_up, up); hop_a(1, y_dn, dn)
-            pass_on(1, y_dn); I(p_own); pass_on(2, y_up); pass_on(3, y); m2(); far_b()
-        if ORDER == 3:
-            I(p_far, False); m0(); swap_near_far(); rest(); T(y_far, 0); r1(); I(p_up); I(p_dn); m1_free(); T(y_dn, 1); free_a(1, y_dn, dn)
-            T(y_up, 2); free_a(0, y_up, up); T(y, 3); m1(); pass_on(0, y_far); hop_a(0, y_up, up); hop_a(1, y_dn, dn)
-            pass_on(1, y_dn); pass_on(2, y_up); I(p_own); far_b(); pass_on(3, y); m2()
 
         lane = lax.broadcasted_iota(jnp.int32, (8, TOK), 1)
 
@@ -646,17 +633,39 @@
             scal_z[line_rank] = scal_send[0]
             return log_img
 
-        if SCAL == 0:
-            log_img = scalars()
+        def second_step(log_img):
+            landed(scal_z.at[0:15], r_sz.at[0])
+            line_sum = jnp.sum(scal_z[...], axis=0)
+            scal_send[1] = jnp.where(lane == 4, log_img, line_sum)
+            for peer in plane_peers:
+                send("all", scal_send.at[1], scal_p.at[plane_rank], r_sp.at[0], peer)
+            scal_p[plane_rank] = scal_send[1]
+            return line_sum
+
+        S1, S2 = scalars, second_step
+        if ORDER == 1:
+            I(p_far, False); m0(); swap_near_far(); rest(); T(y_far, 0); r1(); log_img = S1(); I(p_up); I(p_dn); T(y_dn, 1); m1_free()
+            free_a(1, y_dn, dn); T(y_up, 2); free_a(0, y_up, up); m1(); pass_on(0, y_far); hop_a(0, y_up, up); hop_a(1, y_dn, dn)
+            T(y, 3); pass_on(1, y_dn); pass_on(2, y_up); line_sum = S2(log_img); I(p_own); far_b(); pass_on(3, y); m2()
+        if ORDER == 2:
+            rest(); T(y_far, 0); r1(); I(p_far, False); m0(); swap_near_far(); log_img = S1(); I(p_up); T(y_dn, 1); I(p_dn); m1_free()
+            free_a(1, y_dn, dn); T(y_up, 2); free_a(0, y_up, up); pass_on(0, y_far); m1(); hop_a(0, y_up, up); hop_a(1, y_dn, dn)
+            T(y, 3); pass_on(1, y_dn); line_sum = S2(log_img); pass_on(2, y_up); I(p_own); far_b(); pass_on(3, y); m2()
+        if ORDER == 3:
+            I(p_far, False); m0(); swap_near_far(); rest(); T(y_far, 0); r1(); T(y_dn, 1); log_img = S1(); I(p_up); I(p_dn); m1_free()
+            T(y_up, 2); pass_on(0, y_far); m1(); free_a(1, y_dn, dn); free_a(0, y_up, up); hop_a(0, y_up, up); hop_a(1, y_dn, dn)
+            T(y, 3); pass_on(1, y_dn); pass_on(2, y_up); line_sum = S2(log_img); far_b(); I(p_own); pass_on(3, y); m2()
+        if ORDER == 4:
+            I(p_far, False); m0(); swap_near_far(); rest(); T(y_far, 0); r1(); I(p_up); I(p_dn); T(y_dn, 1); m1_free(); T(y_up, 2)
+            log_img = S1(); pass_on(0, y_far); m1(); hop_a(0, y_up, up); hop_a(1, y_dn, dn); free_a(1, y_dn, dn); free_a(0, y_up, up)
+            T(y, 3); pass_on(1, y_dn); pass_on(2, y_up); I(p_own); far_b(); pass_on(3, y); line_sum = S2(log_img); m2()
+
         add_sibling(p_own)
 
         @when("odd")
         def _():
             fin_send[...] = image_part[z, c].astype(bf16)
             send("odd", fin_send, fin_recv.at[2], r_fin.at[2, 0], partner)
-
-        if SCAL == 1:
-            log_img = scalars()
 
         for part in range(2):
             for way in range(2):
@@ -682,18 +691,6 @@
             for q in range(2):
                 send("even", stage(y * 2 + q, xo), ra_fin.at[xh, 0], r_af.at[xh, 0], across[q])
 
-        def second_step():
-            landed(scal_z.at[0:15], r_sz.at[0])
-            line_sum = jnp.sum(scal_z[...], axis=0)
-            scal_send[1] = jnp.where(lane == 4, log_img, line_sum)
-            for peer in plane_peers:
-                send("all", scal_send.at[1], scal_p.at[plane_rank], r_sp.at[0], peer)
-            scal_p[plane_rank] = scal_send[1]
-            return line_sum
-
-        if SCAL2 == 1:
-            line_sum = second_step()
-
         for h in (1, 0):
             ring_send(3, h, True)
             ring_send(3, 1 - h, False)
@@ -704,15 +701,16 @@
                 landed(ra_x.at[1 - q], r_ax.at[1 - q])
                 add(y * 2 + q, xh, ra_x[1 - q])
                 send("even", stage(y * 2 + q, xh), ra_fin.at[xh, 1], r_af.at[xh, 1], across[q])
-
-        if SCAL2 == 0:
-            line_sum = second_step()
 
         def finish(part, grads):
             unit32, lengths = normal(part)
             grads = scale * grads
             inner = jnp.sum(unit32 * grads, axis=1, keepdims=True)
-            out_ref[0, part] = ((grads - unit32 * inner) / lengths).astype(bf16)
+            result = (grads - unit32 * inner) / lengths
+            if OUTF:
+                out_ref[part] = result
+            else:
+                out_ref[0, part] = result.astype(bf16)
 
         @when("odd")
         def _():
@@ -774,7 +772,7 @@
         ((HALF, D), bf16),
         ((8, 2, HALF, D), bf16),
         ((8, TOK, D), bf16),
-        ((16, 8, TOK), jnp.int32),
+        ((16, TOK), f32),
         ((8, TOK, WIDE), f32),
         ((8, TOK, WIDE), bf16),
         ((8, TOK, D), f32),
@@ -799,7 +797,7 @@
         ((8, TOK), jnp.int32),
         ((8, TOK), f32),
         ((4, 8, TOK), f32),
-        ((16, 8, TOK), f32),
+        ((16, 16, TOK), f32),
         ((16, 8, TOK), f32),
         ((8, TOK), f32),
         ((2, 8, TOK), f32),
@@ -809,13 +807,13 @@
         ((3, HALF, D), bf16),
     ]
     sems = [
-        (1,), (SENDS,), (8, 4), (8, 4), (8,), (1,), (4,), (1,), (1,), (1,), (1,),
-        (2,), (2, 2), (2,), (2, 2), (4, 2, 2), (4, 2), (2,), (2, 2), (4,), (4, 2), (4, 2), (3, 2), (4,), (2, 2),
+        (1,), (SENDS,), (8, 4), (8, WAVES), (8,), (WAVES,), (1,), (1,), (1,), (1,),
+        (2,), (2, 2), (2,), (2, 2), (4, 2, 2), (4, 2), (2,), (2, 2), (4,), (4, 2), (4, 2), (3, 2), (WAVES,), (2, 2),
     ]
-    return pl.pallas_call(
+    grads, loss, scale_grad = pl.pallas_call(
         kernel,
         out_shape=(
-            jax.ShapeDtypeStruct((1, TOK, D), bf16),
+            jax.ShapeDtypeStruct((TOK, D), f32) if OUTF else jax.ShapeDtypeStruct((1, TOK, D), bf16),
             jax.ShapeDtypeStruct((1,), f32),
             jax.ShapeDtypeStruct((1,), f32),
         ),
@@ -832,6 +830,7 @@
         embeddings,
         pair.reshape(1, TOK),
     )
+    return (grads.astype(bf16)[None] if OUTF else grads), loss, scale_grad
 
 
 def solution(mesh):

time: 73.8 us -> 74.5 us (level)
  other arithmetic: 0 us -> 1.73 us
  local copies, waits for them, and re-layouts: 1.65 us -> 0 us
    broadcast_in_dim x0 -> x1, other arithmetic: none -> 1.73 us  [body(): return (grads.astype(bf16)[None] if OUTF else grads, loss, scale_grad)]
    unnamed x1 -> x0, local copies, waits for them, and re-layouts: 1.65 us -> none
where the time goes in v5:
time: 74.5 us; the launch traced here: 74.3 us
  Pallas kernels  67.7 us (91%)
  between operations  4.86 us (7%)
  other arithmetic  1.73 us (2%)
    pallas_call x1, Pallas kernels, body(): pl.pallas_call(kernel, out_shape=(jax.ShapeDtypeStruct((TOK, D), f32) if...  67.7 us
    broadcast_in_dim x1, other arithmetic, body(): return (grads.astype(bf16)[None] if OUTF else grads, loss, scale_grad)  1.73 us

profile of v5, /device:TPU:2, one launch (start us, length us, event | category | flops | bytes accessed | tf_op | source)
XLA Modules:
  0.0 74.3 jit_solution(10785159605621936083)
XLA Ops:
  1.3 67.7 %contrastive.1 = (f32[128,896]{1,0:T(8,128)}, f32[1]{0:T(128)}, f32[1]{0:T(128)}) custom-call(f32[1]{0:T(128)} %bitcast.4.scale_ref, bf16[1,128,896]{2,1,0:T(8,128)(2,1)} %emb_hbm.1, s32[1,128]{1,0:T(1,128)} %bitcast.5), custom_call_target="tpu_custom_call" | custom-call | flops 5637144576 | bytes 1048576 | tf_op jit(solution)/shard_map/contrastive/pallas_call | solution.py:813
  69.0 1.7 %convert_bitcast_fusion = bf16[1,128,896]{2,1,0:T(8,128)(2,1)} fusion(f32[128,896]{1,0:T(8,128)} %get-tuple-element.6), kind=kLoop, calls=%fused_computation | loop fusion | flops 114688 | bytes 688128 | tf_op jit(solution)/shard_map/broadcast_in_dim | solution.py:833

commit v6 on v5

--- a/solution.py
+++ b/solution.py
@@ -20,10 +20,12 @@
 DIRECT = 0
 DRAINS = 0
 ORDER = 4
-OUTF = 1
+HOP3 = 1
+XF = 1
+OUTF = 0
 SCAL = 0
 SCAL2 = 1
-SENDS = 48
+SENDS = 30
 
 
 def device(t, y, xh, z, c):
@@ -33,7 +35,7 @@
 def kernel(
     scale_ref, emb_hbm, pair_ref,
     out_ref, loss_ref, sgrad_ref,
-    emb_ref, own, images, texts, z_msg, exps, weights,
+    emb_ref, unit_ref, length_ref, own, images, texts, z_msg, exps, weights,
     text_part, text_send, ra_one, ra_two, ra_x, ra_fin, rb_odd, rb_even, rb_one, rb_two,
     image_part, image_send, image_sib, image_right, image_left, image_first,
     z_row, e_row, columns, pair_rows, hits, stat_send, z_img_all, z_txt_all, e_sums, scal_send, scal_z, scal_p, fin_send, fin_recv,
@@ -122,11 +124,14 @@
     def normal(part):
         wide = emb_ref[part].astype(f32)
         lengths = jnp.sqrt(jnp.sum(wide * wide, axis=1, keepdims=True) + eps)
-        return wide / lengths, lengths
+        unit32 = wide / lengths
+        unit_ref[part] = unit32
+        length_ref[part] = lengths
+        return unit32.astype(bf16)
 
     lower, upper = slice(0, HALF), slice(HALF, TOK)
-    unit_low = normal(lower)[0].astype(bf16)
-    unit_high = normal(upper)[0].astype(bf16)
+    unit_low = normal(lower)
+    unit_high = normal(upper)
 
     @when("odd")
     def _():
@@ -202,9 +207,13 @@
             def mine(w):
                 return own.at[pl.ds(w * size, size)]
 
+            for w in range(WAVES if XF else 0):
+                send(n, mine(w), piece(z, w), r_x.at[w], partner)
             for w in range(WAVES):
                 isend(n, z, w, zp)
                 isend(n, z, w, zm)
+                if XF:
+                    continue
                 if DIRECT:
                     send(n, mine(w), piece(z, w), r_img.at[z, w], partner_zp)
                     send(n, mine(w), piece(z, w), r_img.at[z, w], partner_zm)
@@ -330,6 +339,8 @@
             tsend(n, y_dn * 2 + xo, 0, up)
             twait(y_up * 2 + xo, 1)
             tsend(n, y_up * 2 + xo, 1, dn)
+            if HOP3:
+                image_hop(n, 3)
             for q in (xh, xo):
                 twait(y_dn * 2 + q, 1)
                 twait(y_up * 2 + q, 0)
@@ -376,9 +387,10 @@
 
         stats(p_own, True)
 
-        @when("odd")
-        def _():
-            image_hop("odd", 3)
+        if not HOP3:
+            @when("odd")
+            def _():
+                image_hop("odd", 3)
 
         for p in (p_up, p_dn):
             siblings(p)
@@ -702,8 +714,20 @@
                 add(y * 2 + q, xh, ra_x[1 - q])
                 send("even", stage(y * 2 + q, xh), ra_fin.at[xh, 1], r_af.at[xh, 1], across[q])
 
+        landed(scal_p.at[0:15], r_sp.at[0])
+        all_sum = jnp.sum(scal_p[...], axis=0)
+
+        def pick(x, k):
+            return jnp.sum(jnp.where(lane[0:1] == k, x[0:1], 0.0))
+
+        log_all = jnp.where(odd, pick(line_sum, 0), pick(all_sum, 4))
+        t_all = jnp.where(odd, pick(all_sum, 2), pick(all_sum, 1))
+        p_all = pick(all_sum, 3)
+        loss_ref[0] = (scale * TOKENS + log_all - p_all) * (1.0 / (2 * TOKENS))
+        sgrad_ref[0] = (t_all - p_all) / scale * (1.0 / (2 * TOKENS))
+
         def finish(part, grads):
-            unit32, lengths = normal(part)
+            unit32, lengths = unit_ref[part], length_ref[part]
             grads = scale * grads
             inner = jnp.sum(unit32 * grads, axis=1, keepdims=True)
             result = (grads - unit32 * inner) / lengths
@@ -744,18 +768,8 @@
                 fin_recv[0].astype(f32) + fin_recv[1].astype(f32) + fin_recv[2].astype(f32),
             )
 
-        landed(scal_p.at[0:15], r_sp.at[0])
-        all_sum = jnp.sum(scal_p[...], axis=0)
-
-        def pick(x, k):
-            return jnp.sum(jnp.where(lane[0:1] == k, x[0:1], 0.0))
-
-        log_all = jnp.where(odd, pick(line_sum, 0), pick(all_sum, 4))
-        t_all = jnp.where(odd, pick(all_sum, 2), pick(all_sum, 1))
-        p_all = pick(all_sum, 3)
-        loss_ref[0] = (scale * TOKENS + log_all - p_all) * (1.0 / (2 * TOKENS))
-        sgrad_ref[0] = (t_all - p_all) / scale * (1.0 / (2 * TOKENS))
-
+
+    assert count[0] <= SENDS, count[0]
     for name in pending:
         if pending[name]:
             @when(name)
@@ -769,6 +783,8 @@
     dma = pltpu.SemaphoreType.DMA
     scratch = [
         ((TOK, D), bf16),
+        ((TOK, D), f32),
+        ((TOK, 1), f32),
         ((HALF, D), bf16),
         ((8, 2, HALF, D), bf16),
         ((8, TOK, D), bf16),

time: 74.5 us -> 71.9 us (0.965)
  Pallas kernels: 67.7 us -> 65.1 us
  other arithmetic: 1.73 us -> 0 us
  local copies, waits for them, and re-layouts: 0 us -> 1.65 us
    pallas_call x1, Pallas kernels: 67.7 us -> 65.1 us  [body(): pl.pallas_call(kernel, out_shape=(jax.ShapeDtypeStruct((TOK, D), f32) if...]
    broadcast_in_dim x1 -> x0, other arithmetic: 1.73 us -> none  [body(): return (grads.astype(bf16)[None] if OUTF else grads, loss, scale_grad)]
    unnamed x0 -> x1, local copies, waits for them, and re-layouts: none -> 1.65 us
where the time goes in v6:
time: 71.9 us; the launch traced here: 71.6 us
  Pallas kernels  65.1 us (91%)
  between operations  4.79 us (7%)
  local copies, waits for them, and re-layouts  1.65 us (2%)
    pallas_call x1, Pallas kernels, body(): pl.pallas_call(kernel, out_shape=(jax.ShapeDtypeStruct((TOK, D), f32) if...  65.1 us
    unnamed x1, local copies, waits for them, and re-layouts  1.65 us

profile of v6, /device:TPU:2, one launch (start us, length us, event | category | flops | bytes accessed | tf_op | source)
XLA Modules:
  0.0 71.6 jit_solution(16140987435452250096)
XLA Ops:
  1.3 65.1 %contrastive.1 = (bf16[1,128,896]{2,1,0:T(8,128)(2,1)}, f32[1]{0:T(128)}, f32[1]{0:T(128)}) custom-call(f32[1]{0:T(128)} %bitcast.2.scale_ref, bf16[1,128,896]{2,1,0:T(8,128)(2,1)} %emb_hbm.1, s32[1,128]{1,0:T(1,128)} %bitcast.3), custom_call_target="tpu_custom_call" | custom-call | flops 5637144576 | bytes 1048576 | tf_op jit(solution)/shard_map/contrastive/pallas_call | solution.py:829
  66.4 1.6 %copy.10 = bf16[1,128,896]{2,1,0:T(8,128)(2,1)} copy(bf16[1,128,896]{2,1,0:T(8,128)(2,1)} %get-tuple-element.6) | data formatting | bytes 458752

commit v7 on v6

--- a/solution.py
+++ b/solution.py
@@ -17,14 +17,6 @@
 MESH = pl.DeviceIdType.MESH
 STEPS = 9
 WAVES = 2
-DIRECT = 0
-DRAINS = 0
-ORDER = 4
-HOP3 = 1
-XF = 1
-OUTF = 0
-SCAL = 0
-SCAL2 = 1
 SENDS = 30
 
 
@@ -207,18 +199,11 @@
             def mine(w):
                 return own.at[pl.ds(w * size, size)]
 
-            for w in range(WAVES if XF else 0):
+            for w in range(WAVES):
                 send(n, mine(w), piece(z, w), r_x.at[w], partner)
             for w in range(WAVES):
                 isend(n, z, w, zp)
                 isend(n, z, w, zm)
-                if XF:
-                    continue
-                if DIRECT:
-                    send(n, mine(w), piece(z, w), r_img.at[z, w], partner_zp)
-                    send(n, mine(w), piece(z, w), r_img.at[z, w], partner_zm)
-                else:
-                    send(n, mine(w), piece(z, w), r_x.at[w], partner)
             to_sibling(n, z)
             image_hop(n, 1)
             for q in range(2):
@@ -248,8 +233,6 @@
                 index = yb * 2 + q
                 twait(index, 2 + xh)
                 tsend(n, index, 2 + xh, across[1 - q])
-            for w in range(WAVES if DIRECT else 0):
-                send(n, mine(w), piece(z, w), r_x.at[w], partner)
             for q in range(2):
                 twait(y_dn * 2 + q, 0)
                 tsend(n, y_dn * 2 + q, 0, up)
@@ -285,20 +268,15 @@
                 tsend(n, mine, e, across[e], "s")
             tsend(n, mine, 2, up, "s")
             tsend(n, mine, 3, dn, "s")
-            if DRAINS > 0:
-                drain(n, "s")
             for e in range(2):
                 tsend(n, mine, 1 - e, across[e], "s")
             tsend(n, mine, 3, up, "s")
             tsend(n, mine, 2, dn, "s")
-            if DRAINS > 1:
-                drain(n, "s")
-            if not DIRECT:
-                for w in range(WAVES):
-                    landed(piece(z, w), r_x.at[w])
-                    isend(n, z, w, zp)
-                    isend(n, z, w, zm)
-                to_sibling(n, z)
+            for w in range(WAVES):
+                landed(piece(z, w), r_x.at[w])
+                isend(n, z, w, zp)
+                isend(n, z, w, zm)
+            to_sibling(n, z)
             for e in range(2):
                 relayed(mine, e)
             tsend(n, mine, 0, up)
@@ -339,8 +317,7 @@
             tsend(n, y_dn * 2 + xo, 0, up)
             twait(y_up * 2 + xo, 1)
             tsend(n, y_up * 2 + xo, 1, dn)
-            if HOP3:
-                image_hop(n, 3)
+            image_hop(n, 3)
             for q in (xh, xo):
                 twait(y_dn * 2 + q, 1)
                 twait(y_up * 2 + q, 0)
@@ -349,10 +326,6 @@
             for ya in (y, y_dn, y_up, y_far):
                 for k in range(2):
                     twait(ya * 2 + xo, 2 + k)
-            if DIRECT:
-                for w in range(WAVES):
-                    landed(piece(z, w), r_x.at[w])
-                to_sibling(n, z)
 
         siblings(p_own)
 
@@ -386,11 +359,6 @@
             e_row[...] = er if first else e_row[...] + er
 
         stats(p_own, True)
-
-        if not HOP3:
-            @when("odd")
-            def _():
-                image_hop("odd", 3)
 
         for p in (p_up, p_dn):
             siblings(p)
@@ -655,22 +623,32 @@
             return line_sum
 
         S1, S2 = scalars, second_step
-        if ORDER == 1:
-            I(p_far, False); m0(); swap_near_far(); rest(); T(y_far, 0); r1(); log_img = S1(); I(p_up); I(p_dn); T(y_dn, 1); m1_free()
-            free_a(1, y_dn, dn); T(y_up, 2); free_a(0, y_up, up); m1(); pass_on(0, y_far); hop_a(0, y_up, up); hop_a(1, y_dn, dn)
-            T(y, 3); pass_on(1, y_dn); pass_on(2, y_up); line_sum = S2(log_img); I(p_own); far_b(); pass_on(3, y); m2()
-        if ORDER == 2:
-            rest(); T(y_far, 0); r1(); I(p_far, False); m0(); swap_near_far(); log_img = S1(); I(p_up); T(y_dn, 1); I(p_dn); m1_free()
-            free_a(1, y_dn, dn); T(y_up, 2); free_a(0, y_up, up); pass_on(0, y_far); m1(); hop_a(0, y_up, up); hop_a(1, y_dn, dn)
-            T(y, 3); pass_on(1, y_dn); line_sum = S2(log_img); pass_on(2, y_up); I(p_own); far_b(); pass_on(3, y); m2()
-        if ORDER == 3:
-            I(p_far, False); m0(); swap_near_far(); rest(); T(y_far, 0); r1(); T(y_dn, 1); log_img = S1(); I(p_up); I(p_dn); m1_free()
-            T(y_up, 2); pass_on(0, y_far); m1(); free_a(1, y_dn, dn); free_a(0, y_up, up); hop_a(0, y_up, up); hop_a(1, y_dn, dn)
-            T(y, 3); pass_on(1, y_dn); pass_on(2, y_up); line_sum = S2(log_img); far_b(); I(p_own); pass_on(3, y); m2()
-        if ORDER == 4:
-            I(p_far, False); m0(); swap_near_far(); rest(); T(y_far, 0); r1(); I(p_up); I(p_dn); T(y_dn, 1); m1_free(); T(y_up, 2)
-            log_img = S1(); pass_on(0, y_far); m1(); hop_a(0, y_up, up); hop_a(1, y_dn, dn); free_a(1, y_dn, dn); free_a(0, y_up, up)
-            T(y, 3); pass_on(1, y_dn); pass_on(2, y_up); I(p_own); far_b(); pass_on(3, y); line_sum = S2(log_img); m2()
+        I(p_far, False)
+        m0()
+        swap_near_far()
+        rest()
+        T(y_far, 0)
+        r1()
+        I(p_up)
+        I(p_dn)
+        T(y_dn, 1)
+        m1_free()
+        T(y_up, 2)
+        log_img = S1()
+        pass_on(0, y_far)
+        m1()
+        hop_a(0, y_up, up)
+        hop_a(1, y_dn, dn)
+        free_a(1, y_dn, dn)
+        free_a(0, y_up, up)
+        T(y, 3)
+        pass_on(1, y_dn)
+        pass_on(2, y_up)
+        I(p_own)
+        far_b()
+        pass_on(3, y)
+        line_sum = S2(log_img)
+        m2()
 
         add_sibling(p_own)
 
@@ -689,6 +667,21 @@
         def _():
             for k in range(2):
                 send("odd", stage(y * 2 + xo, k), ra_x.at[xh], r_ax.at[xh], across[k])
+
+        @when("even")
+        def _():
+            for q in range(2):
+                send("even", stage(y * 2 + q, xo), ra_fin.at[xh, 0], r_af.at[xh, 0], across[q])
+
+        def m3():
+            for h in (1, 0):
+                ring_send(3, h, True)
+                ring_send(3, 1 - h, False)
+
+        m3()
+
+        @when("odd")
+        def _():
             take_b(1, y_dn)
             take_b(2, y_up)
             send("odd", stage(y_up * 2 + xh, 3), rb_two.at[0, 0], r_b2.at[0, 0], up)
@@ -701,15 +694,6 @@
         @when("even")
         def _():
             for q in range(2):
-                send("even", stage(y * 2 + q, xo), ra_fin.at[xh, 0], r_af.at[xh, 0], across[q])
-
-        for h in (1, 0):
-            ring_send(3, h, True)
-            ring_send(3, 1 - h, False)
-
-        @when("even")
-        def _():
-            for q in range(2):
                 landed(ra_x.at[1 - q], r_ax.at[1 - q])
                 add(y * 2 + q, xh, ra_x[1 - q])
                 send("even", stage(y * 2 + q, xh), ra_fin.at[xh, 1], r_af.at[xh, 1], across[q])
@@ -731,10 +715,7 @@
             grads = scale * grads
             inner = jnp.sum(unit32 * grads, axis=1, keepdims=True)
             result = (grads - unit32 * inner) / lengths
-            if OUTF:
-                out_ref[part] = result
-            else:
-                out_ref[0, part] = result.astype(bf16)
+            out_ref[0, part] = result.astype(bf16)
 
         @when("odd")
         def _():
@@ -829,7 +810,7 @@
     grads, loss, scale_grad = pl.pallas_call(
         kernel,
         out_shape=(
-            jax.ShapeDtypeStruct((TOK, D), f32) if OUTF else jax.ShapeDtypeStruct((1, TOK, D), bf16),
+            jax.ShapeDtypeStruct((1, TOK, D), bf16),
             jax.ShapeDtypeStruct((1,), f32),
             jax.ShapeDtypeStruct((1,), f32),
         ),
@@ -846,7 +827,7 @@
         embeddings,
         pair.reshape(1, TOK),
     )
-    return (grads.astype(bf16)[None] if OUTF else grads), loss, scale_grad
+    return grads, loss, scale_grad
 
 
 def solution(mesh):

time: 71.9 us -> 71.8 us (level)
  no operation moved by 1% of the time
where the time goes in v7:
time: 71.8 us; the launch traced here: 71.6 us
  Pallas kernels  65.1 us (91%)
  between operations  4.79 us (7%)
  local copies, waits for them, and re-layouts  1.65 us (2%)
    pallas_call x1, Pallas kernels, body(): pl.pallas_call(kernel, out_shape=(jax.ShapeDtypeStruct((1, TOK, D), bf16)...  65.1 us
    unnamed x1, local copies, waits for them, and re-layouts  1.65 us

profile of v7, /device:TPU:2, one launch (start us, length us, event | category | flops | bytes accessed | tf_op | source)
XLA Modules:
  0.0 71.6 jit_solution(1289820409249361223)
XLA Ops:
  1.3 65.1 %contrastive.1 = (bf16[1,128,896]{2,1,0:T(8,128)(2,1)}, f32[1]{0:T(128)}, f32[1]{0:T(128)}) custom-call(f32[1]{0:T(128)} %bitcast.2.scale_ref, bf16[1,128,896]{2,1,0:T(8,128)(2,1)} %emb_hbm.1, s32[1,128]{1,0:T(1,128)} %bitcast.3), custom_call_target="tpu_custom_call" | custom-call | flops 5637144576 | bytes 1048576 | tf_op jit(solution)/shard_map/contrastive/pallas_call | solution.py:810
  66.4 1.6 %copy.10 = bf16[1,128,896]{2,1,0:T(8,128)(2,1)} copy(bf16[1,128,896]{2,1,0:T(8,128)(2,1)} %get-tuple-element.6) | data formatting | bytes 458752

commit v8 on v7

--- a/solution.py
+++ b/solution.py
@@ -109,7 +109,7 @@
     fetch = pltpu.make_async_copy(emb_hbm.at[0], emb_ref, s_in.at[0])
     fetch.start()
     barrier = pltpu.get_barrier_semaphore()
-    for peer in (up, dn, zp, zm, sibling, across[0], across[1], partner_zp, partner_zm):
+    for peer in (up, dn, zp, zm, sibling, across[0], across[1]):
         pl.semaphore_signal(barrier, inc=1, device_id=peer, device_id_type=MESH)
     fetch.wait()
 
@@ -136,7 +136,7 @@
         own[...] = unit_high
 
     z_msg[8:16, :] = jnp.broadcast_to(pair_ref[...], (8, TOK)).astype(f32)
-    pl.semaphore_wait(barrier, 9)
+    pl.semaphore_wait(barrier, 7)
 
     def rows(index, quarter):
         return texts.at[index, pl.ds(quarter * QUART, QUART)]

time: 71.8 us -> 71.8 us (level)
  no operation moved by 1% of the time
where the time goes in v8:
time: 71.8 us; the launch traced here: 71.6 us
  Pallas kernels  65.2 us (91%)
  between operations  4.79 us (7%)
  local copies, waits for them, and re-layouts  1.65 us (2%)
    pallas_call x1, Pallas kernels, body(): pl.pallas_call(kernel, out_shape=(jax.ShapeDtypeStruct((1, TOK, D), bf16)...  65.2 us
    unnamed x1, local copies, waits for them, and re-layouts  1.65 us

profile of v8, /device:TPU:2, one launch (start us, length us, event | category | flops | bytes accessed | tf_op | source)
XLA Modules:
  0.0 71.6 jit_solution(16733980923418665219)
XLA Ops:
  1.3 65.2 %contrastive.1 = (bf16[1,128,896]{2,1,0:T(8,128)(2,1)}, f32[1]{0:T(128)}, f32[1]{0:T(128)}) custom-call(f32[1]{0:T(128)} %bitcast.2.scale_ref, bf16[1,128,896]{2,1,0:T(8,128)(2,1)} %emb_hbm.1, s32[1,128]{1,0:T(1,128)} %bitcast.3), custom_call_target="tpu_custom_call" | custom-call | flops 5637144576 | bytes 1048576 | tf_op jit(solution)/shard_map/contrastive/pallas_call | solution.py:810
  66.4 1.6 %copy.10 = bf16[1,128,896]{2,1,0:T(8,128)(2,1)} copy(bf16[1,128,896]{2,1,0:T(8,128)(2,1)} %get-tuple-element.6) | data formatting | bytes 458752
